TPU v7x, 128 devices: a whole 4x4x4 slice. The times are simulated.
128 devices in a mesh: lat: 8 (over x, core), lon: 16 (over y, z).
Axes of the slice: x: 4, y: 4, z: 4, core: 2. Of those that a mesh axis runs over, the one named last changes fastest.
Arguments:
- op_blocks: bfloat16 [16384, 128, 128], P(('lat', 'lon')), may hold values from -0.5 to 0.5
- innovations: bfloat16 [16384, 16, 128], P(('lat', 'lon')), may hold values from -6 to 6
- obs_tiles: int32 [16384], P(('lat', 'lon')), may hold values from 0 to 127, as said below
- col_blocks: int32 [16384], P(('lat', 'lon')), may hold values from 0 to 255
- time_slots: int32 [16384], P(('lat', 'lon')), may hold values from 0 to 3
- obs_count: int32 [128], P(('lat', 'lon')), may hold values from 96 to 128, as said below
- courant: float32 [5, 512, 8192], P(None, 'lat', 'lon'), may hold values from 0.05 to 0.3
- later_adjoint: float32 [16, 512, 8192], P(None, 'lat', 'lon'), may hold values from -6 to 6
Outputs:
- gradient: float32 [16, 512, 8192], P(None, 'lat', 'lon')
Inputs may be any that keep to these rules, and one draw needn't show every extreme that they name: `obs_tiles`: tiles are numbered with the latitude tile slowest. Among the used blocks of one device at most 2 name one tile, and in every draw some tile is named exactly 2 times by the used blocks of every device. `obs_count`: some device uses all 128 of its blocks.
All inputs are finite; a program needn't handle non-finite values.
Results may differ from a plain program's by a relative error of at most 0.0003.
Values may be sent and summed in bfloat16 or wider, within the bound.
No kernel may reach another device: no remote copies, remote signals or barrier semaphores. Data moves between devices by JAX's collectives and lax.ppermute only.
A program may use at most 128 MiB of HBM per device.

v0:
```python
import jax
import jax.numpy as jnp
from jax import lax
from jax.experimental import pallas as pl
from jax.experimental.pallas import tpu as pltpu
from jax.sharding import PartitionSpec as P

STEPS = 4
LEV = 16
LANE = 128
NOTES = 2 * LEV
ROWS = NOTES + 8
PIECES = 4
OFFSETS = (0, 4, 9, 13)
HALO = 4
WEIGHTS = 5
PACK = 32
LIMIT = 32766.0
F32 = jnp.float32
I32 = jnp.int32
I16 = jnp.int16


def any_spec():
    return pl.BlockSpec(memory_space=pltpu.HBM)


def in_hbm(array):
    return pltpu.with_memory_space_constraint(array, pltpu.HBM)


def vmem_spec():
    return pl.BlockSpec(memory_space=pltpu.VMEM)


def params(mib):
    return pltpu.CompilerParams(vmem_limit_bytes=mib * 2**20)


def lanes8():
    return lax.broadcasted_iota(I32, (8, LANE), 1)


def sublanes8():
    return lax.broadcasted_iota(I32, (8, LANE), 0)


def aligned(index, by):
    return pl.multiple_of(index * by, by)


def log2_of(size):
    bits = size.bit_length() - 1
    assert size == 1 << bits
    return bits


def scale_of(code):
    return jnp.exp2(code * (1.0 / 16.0)) * (1.0 / LIMIT)


def shared_groups(value):
    value = value + pltpu.roll(value, 32, 1)
    return value + pltpu.roll(value, 64, 1)


def own_group():
    return lanes8() // 32 == sublanes8() % 4


def contribution_kernel(
    lat_cells, per_row, lon_tiles,
    count, tiles_hbm, cols_hbm, slots_hbm, op_hbm, inn_hbm, field_hbm, courant_hbm,
    sent, to_east, to_west,
    pay, op, inn, strip, meta, tiles, cols, slots, arrived, sems,
):
    blocks = op.shape[0]
    devices = lax.axis_size("lat") * lon_tiles
    parts = 4
    chunk = blocks // parts
    small = [
        pltpu.make_async_copy(a, b, sems.at[k])
        for k, (a, b) in enumerate(
            ((tiles_hbm, tiles), (cols_hbm, cols), (slots_hbm, slots))
        )
    ]
    inn_copy = pltpu.make_async_copy(inn_hbm, inn, sems.at[4])
    copies = []
    for part in range(parts):
        at = pl.ds(part * chunk, chunk)
        copies.append(pltpu.make_async_copy(op_hbm.at[at], op.at[at], sems.at[5 + part]))
    strips = []
    rows = field_hbm.shape[0]
    extra = courant_hbm.shape[0]
    for side, lane_at in enumerate((0, (per_row - 1) * LANE)):
        strips.append(
            pltpu.make_async_copy(
                field_hbm.at[:, pl.ds(lane_at, LANE)], strip.at[side, pl.ds(0, rows)],
                sems.at[5 + parts + 2 * side],
            )
        )
        strips.append(
            pltpu.make_async_copy(
                courant_hbm.at[:, pl.ds(lane_at, LANE)], strip.at[side, pl.ds(rows, extra)],
                sems.at[6 + parts + 2 * side],
            )
        )
    for copy in small + strips + [inn_copy] + copies:
        copy.start()

    def clear(d, _):
        arrived[d] = 0
        meta[pl.ds(aligned(d, 8), 8), :] = jnp.zeros((8, LANE), I32)
        return 0

    lax.fori_loop(0, devices + 1, clear, 0, unroll=8)
    lane8 = lanes8()
    lane = lane8[0:1]
    own = own_group()

    for copy in strips:
        copy.wait()
    total = (rows + extra) // 8
    for v in range(-(-total // PACK)):
        east = jnp.zeros((8, LANE), F32)
        west = jnp.zeros((8, LANE), F32)
        for k in range(min(PACK, total - v * PACK)):
            at = pl.ds(8 * (v * PACK + k), 8)
            here = lane8 // HALO == k
            west = jnp.where(here, pltpu.roll(strip[0, at, :], HALO * k, 1), west)
            east = jnp.where(here, pltpu.roll(strip[1, at, :], (HALO * k + HALO) % LANE, 1), east)
        to_east[pl.ds(8 * v, 8), :] = east
        to_west[pl.ds(8 * v, 8), :] = west

    for copy in small:
        copy.wait()
    used = count[0]
    me = lax.axis_index("lat") * lon_tiles + lax.axis_index("lon")
    seat = 8 * (me % 16)
    row_bits = log2_of(per_row)

    def one(j):
        repeat = jnp.where(j < used, 0, 1)
        j = jnp.minimum(j, used - 1)
        dest = tiles[j]
        col = cols[j]
        slot = slots[j]
        nth = jnp.minimum(arrived[dest] - repeat, 1)
        arrived[dest] = nth + 1
        row = col >> row_bits
        at_col = col & (per_row - 1)
        x = jnp.dot(inn[j], op[j], preferred_element_type=F32)
        largest = jnp.max(jnp.abs(x), axis=0, keepdims=True)
        code = jnp.floor(16.0 * jnp.log2(jnp.maximum(largest, 2.0**-100))) + 2.0
        q = jnp.round(x * (1.0 / scale_of(code)))
        pay[dest, pl.ds(pl.multiple_of(nth * LEV, LEV), LEV), :] = q.astype(I32).astype(I16)
        base = aligned(dest, 8)
        meta[pl.ds(base + nth, 1), :] = code.astype(I32)
        rim = (row < slot) | (row >= lat_cells - slot)
        target = (slot * lat_cells + row) * per_row + at_col + 1
        note = jnp.where(lane == seat + 6, 1, target)
        rim_seat = jnp.where(rim, seat + 6, LANE)
        pltpu.store(
            meta.at[pl.ds(base + 5, 1), :], note, mask=(lane == seat + nth) | (lane == rim_seat)
        )
        at_east = at_col == per_row - 1
        near = (at_east | (at_col == 0)) & (slot > 0)
        lon = dest & (lon_tiles - 1)
        other = jnp.where(at_east, lon + 1, lon + lon_tiles - 1) & (lon_tiles - 1)
        beside = jnp.where(near, dest - lon + other, devices)
        piece = nth + jnp.where(at_east, 2, 0)
        first = jnp.where(at_east, LANE - 3, 0)
        offset = jnp.where(at_east, 9, 0) + 4 * nth
        shift = (offset - first) & (LANE - 1)
        wanted = (lane8 >= first) & (lane8 < first + 3)
        mixed = pltpu.roll(jnp.where(wanted, q[:8], 0.0), shift, 1) + pltpu.roll(
            jnp.where(wanted, q[8:], 0.0), (shift + 16) & (LANE - 1), 1
        )
        mixed = jnp.where(own, shared_groups(mixed), 0.0)
        mixed = mixed + pltpu.roll(mixed, 1, 0)
        mixed = (mixed + pltpu.roll(mixed, 2, 0)).astype(I32)
        spot = lane & 15
        here = (spot >= offset) & (spot < offset + 3)
        base = aligned(beside, 8)
        pltpu.store(meta.at[pl.ds(base + 2, 1), :], mixed[3:4], mask=here)
        pltpu.store(meta.at[pl.ds(base + 3, 1), :], mixed[7:8], mask=here)
        turned = pltpu.roll(jnp.broadcast_to(code, (8, LANE)), shift, 1)[0:1].astype(I32)
        pltpu.store(meta.at[pl.ds(base + 4, 1), :], turned, mask=here & (lane < 16))
        note = jnp.where(lane >= seat + 6, 1, slot * lat_cells + row + 1)
        pltpu.store(
            meta.at[pl.ds(base + 5, 1), :], note,
            mask=(lane == seat + 2 + piece) | (lane == seat + 7) | (lane == rim_seat),
        )

    inn_copy.wait()
    for part in range(parts):
        copies[part].wait()

        def some(j, _):
            one(j)
            return 0

        lax.fori_loop(part * chunk, (part + 1) * chunk, some, 0, unroll=8)

    def settle(d, _):
        pay[d, pl.ds(NOTES, 8), :] = meta[pl.ds(aligned(d, 8), 8), :].astype(I16)
        return 0

    lax.fori_loop(0, devices, settle, 0, unroll=8)
    out_copy = pltpu.make_async_copy(pay, sent, sems.at[0])
    out_copy.start()
    out_copy.wait()


def contributions(op_blocks, innovations, obs_tiles, col_blocks, time_slots, obs_count, fields, courant, lat_cells, per_row, lon_tiles, devices):
    blocks = op_blocks.shape[0]
    packed = 8 * -(-(fields.shape[0] + courant.shape[0]) // (8 * PACK))
    strip_rows = fields.shape[0] + courant.shape[0]

    def kernel(*refs):
        contribution_kernel(lat_cells, per_row, lon_tiles, *refs)

    return pl.pallas_call(
        kernel,
        out_shape=[
            pltpu.HBM((devices, ROWS, LANE), I16),
            jax.ShapeDtypeStruct((packed, LANE), F32),
            jax.ShapeDtypeStruct((packed, LANE), F32),
        ],
        in_specs=[pl.BlockSpec(memory_space=pltpu.SMEM)] + [any_spec()] * 7,
        out_specs=[any_spec()] + [vmem_spec()] * 2,
        scratch_shapes=[
            pltpu.VMEM((devices, ROWS, LANE), I16),
            pltpu.VMEM(op_blocks.shape, op_blocks.dtype),
            pltpu.VMEM(innovations.shape, innovations.dtype),
            pltpu.VMEM((2, strip_rows, LANE), F32),
            pltpu.VMEM((8 * (devices + 1), LANE), I32),
            pltpu.SMEM(obs_tiles.shape, I32),
            pltpu.SMEM(col_blocks.shape, I32),
            pltpu.SMEM(time_slots.shape, I32),
            pltpu.SMEM((devices + 1,), I32),
            pltpu.SemaphoreType.DMA((13,)),
        ],
        compiler_params=params(16),
        cost_estimate=pl.CostEstimate(
            flops=2 * blocks * LEV * LANE * LANE, bytes_accessed=6 * 2**20, transcendentals=0
        ),
        name="contributions",
    )(
        obs_count, *map(in_hbm, (obs_tiles, col_blocks, time_slots, op_blocks, innovations, fields, courant))
    )


def ready_kernel(
    lat_cells, per_row, field_hbm, courant_hbm, first_hbm, spread_hbm, lat_hbm,
    first, spread, lat_rows, planes, cplanes, sems,
):
    copies = []
    for c in range(per_row):
        at = pl.ds(c * LANE, LANE)
        copies.append(pltpu.make_async_copy(field_hbm.at[:, at], planes.at[c], sems.at[2 * c]))
        copies.append(pltpu.make_async_copy(courant_hbm.at[:, at], cplanes.at[c], sems.at[2 * c + 1]))
    for copy in copies:
        copy.start()
    for copy in copies:
        copy.wait()

    def widen(g, _):
        for c in range(per_row):
            for d in range(WEIGHTS):
                eight = cplanes[c, pl.ds(pl.multiple_of(d * lat_cells + 8 * g, 8), 8), :]
                for k in range(8):
                    at = pl.ds(pl.multiple_of(((8 * g + k) * WEIGHTS + d) * 8, 8), 8)
                    spread[at, pl.ds(c * LANE, LANE)] = jnp.broadcast_to(eight[k : k + 1], (8, LANE))
        return 0

    lax.fori_loop(0, lat_cells // 8, widen, 0)
    spread_out = pltpu.make_async_copy(spread, spread_hbm.at[:, pl.ds(0, per_row * LANE)], sems.at[0])
    spread_out.start()
    parts = [(h, c) for h in range(LEV // 8) for c in range(per_row)]

    def row_of(i):
        return {
            (h, c): planes[c, pl.ds(8 * h * lat_cells + i, 8, stride=lat_cells), :] for h, c in parts
        }

    def finish(i, total, h, c):
        first[pl.ds(aligned(i, LEV) + 8 * h, 8), pl.ds(c * LANE, LANE)] = total

    for side, i in enumerate((0, lat_cells - 1)):
        row = row_of(i)
        for h, c in parts:
            lat_rows[pl.ds(LEV * side + 8 * h, 8), pl.ds(c * LANE, LANE)] = row[h, c]
    sweep(lat_cells, per_row, spread, row_of, None, finish, wrap=True)
    outs = [
        pltpu.make_async_copy(first, first_hbm, sems.at[1]),
        pltpu.make_async_copy(lat_rows, lat_hbm.at[:, pl.ds(0, per_row * LANE)], sems.at[2]),
    ]
    for out in outs:
        out.start()
    for out in outs + [spread_out]:
        out.wait()


def sweep(lat_cells, tiles, spread, row_of, force_of, finish, group_rows=8, wrap=False):
    lane = lanes8()
    parts = [(h, c) for h in range(LEV // 8) for c in range(tiles)]

    def weight_of(i, d):
        at = pl.ds(pl.multiple_of((i * WEIGHTS + d) * 8, 8), 8)
        return [spread[at, pl.ds(c * LANE, LANE)] for c in range(tiles)]

    def one_row(i, before, mine, after):
        center, east, west, south = (weight_of(i, d) for d in range(4))
        north = weight_of(i + 1, 4) if after is not None else None
        handed = {}
        for h in range(LEV // 8):
            up = [pltpu.roll(east[c] * mine[h, c], 1, 1) for c in range(tiles)]
            dn = [pltpu.roll(west[c] * mine[h, c], LANE - 1, 1) for c in range(tiles)]
            for c in range(tiles):
                total = center[c] * mine[h, c]
                left = 0.0 if wrap and c == 0 else up[c - 1]
                right = 0.0 if wrap and c == tiles - 1 else dn[(c + 1) % tiles]
                total = total + jnp.where(lane == 0, left, up[c])
                total = total + jnp.where(lane == LANE - 1, right, dn[c])
                if force_of is not None:
                    total = total + force_of(i, h, c)
                if before is not None:
                    total = total + before[h, c]
                if after is not None:
                    total = total + north[c] * after[h, c]
                handed[h, c] = south[c] * mine[h, c]
                finish(i, total, h, c)
            if wrap:
                seed = jnp.where(lane == 0, up[tiles - 1], jnp.where(lane == LANE - 1, dn[0], 0.0))
                finish(i, seed, h, tiles)
        return handed

    def rows(first, before, mine, number, ends):
        for k in range(number):
            after = None if ends and k == number - 1 else row_of(first + k + 1)
            before = one_row(first + k, before, mine, after)
            mine = after
        return before, mine

    def group(g, carry):
        before, mine = (dict(zip(parts, values)) for values in carry)
        before, mine = rows(g * group_rows, before, mine, group_rows, False)
        return tuple(before[p] for p in parts), tuple(mine[p] for p in parts)

    nothing = tuple(jnp.zeros((8, LANE), F32) for _ in parts)
    first = row_of(0)
    carry = lax.fori_loop(
        0, lat_cells // group_rows - 1, group, (nothing, tuple(first[p] for p in parts))
    )
    before, mine = (dict(zip(parts, values)) for values in carry)
    rows(lat_cells - group_rows, before, mine, group_rows, True)


def ready(fields, courant, lat_cells, per_row):
    wide = (per_row + 1) * LANE
    lon_cells = per_row * LANE

    def kernel(*refs):
        ready_kernel(lat_cells, per_row, *refs)

    return pl.pallas_call(
        kernel,
        out_shape=[
            pltpu.HBM((lat_cells * LEV, wide), F32),
            pltpu.HBM((lat_cells * WEIGHTS * 8, wide), F32),
            pltpu.HBM((2 * LEV, wide), F32),
        ],
        in_specs=[any_spec()] * 2,
        out_specs=[any_spec()] * 3,
        scratch_shapes=[
            pltpu.VMEM((lat_cells * LEV, wide), F32),
            pltpu.VMEM((lat_cells * WEIGHTS * 8, lon_cells), F32),
            pltpu.VMEM((2 * LEV, lon_cells), F32),
            pltpu.VMEM((per_row, fields.shape[0], LANE), F32),
            pltpu.VMEM((per_row, courant.shape[0], LANE), F32),
            pltpu.SemaphoreType.DMA((2 * per_row,)),
        ],
        compiler_params=params(16),
        cost_estimate=pl.CostEstimate(flops=10**7, bytes_accessed=12 * 2**20, transcendentals=0),
        name="first_step",
    )(in_hbm(fields), in_hbm(courant))


def place_kernel(
    lat_cells, per_row, got, east_halo, west_halo, first_hbm, spread_hbm, lat_hbm,
    force, south, north, lat_rows, spread,
    table_v, wrap_g, wrap_c, table, sems,
):
    wide = (per_row + 1) * LANE
    lon_cells = per_row * LANE
    sources = got.shape[0]
    row_bits = log2_of(per_row)
    top = (STEPS - 1) * lat_cells
    main = pl.ds(0, lon_cells)
    first_copy = pltpu.make_async_copy(first_hbm, force.at[pl.ds(top * LEV, lat_cells * LEV)], sems.at[0])
    lat_copy = pltpu.make_async_copy(lat_hbm.at[:, main], lat_rows.at[:, main], sems.at[1])
    spread_copy = pltpu.make_async_copy(spread_hbm.at[:, main], spread.at[:, main], sems.at[2])
    for copy in (first_copy, lat_copy, spread_copy):
        copy.start()
    for r in range(sources // 16):

        def gather(s, total, r=r):
            return total + got[16 * r + s, pl.ds(NOTES, 8), :].astype(I32)

        total = lax.fori_loop(0, 16, gather, jnp.zeros((8, LANE), I32), unroll=16)
        table_v[pl.ds(r, 1), :] = total[5:6]
    table_copy = pltpu.make_async_copy(table_v, table, sems.at[3])
    table_copy.start()

    def clear(r, _):
        force[pl.ds(aligned(r, LEV), LEV), :] = jnp.zeros((LEV, wide), F32)
        return 0

    lax.fori_loop(0, top, clear, 0, unroll=4)
    lane8 = lanes8()
    rows = wrap_g.shape[0] // 8
    extra = wrap_c.shape[0] // 8
    for n in range(rows + extra):
        v, k = divmod(n, PACK)
        at = pl.ds(8 * v, 8)
        low = pltpu.roll(east_halo[at, :], (-HALO * k) % LANE, 1)
        high = pltpu.roll(west_halo[at, :], (-HALO * k - HALO) % LANE, 1)
        wrap = jnp.where(lane8 < HALO, low, jnp.where(lane8 >= LANE - HALO, high, 0.0))
        if n < rows:
            wrap_g[pl.ds(8 * n, 8), :] = wrap
        else:
            wrap_c[pl.ds(8 * (n - rows), 8), :] = wrap
    last = pl.ds(lon_cells, LANE)
    for g in range(lat_cells // 8):
        for d in range(WEIGHTS):
            eight = wrap_c[pl.ds(d * lat_cells + 8 * g, 8), :]
            for k in range(8):
                spread[pl.ds(((8 * g + k) * WEIGHTS + d) * 8, 8), last] = jnp.broadcast_to(
                    eight[k : k + 1], (8, LANE)
                )
    first_copy.wait()

    def wrap_row(i, h):
        return wrap_g[pl.ds(8 * h * lat_cells + i, 8, stride=lat_cells), :]

    def weight(i, d):
        return spread[pl.ds(pl.multiple_of((i * WEIGHTS + d) * 8, 8), 8), last]

    def wrap_step(i, carry):
        center, east, west, south_w = (weight(i, d) for d in range(4))
        north_w = jnp.where(i < lat_cells - 1, weight(jnp.minimum(i + 1, lat_cells - 1), 4), 0.0)
        handed = []
        for h in range(LEV // 8):
            before, mine = carry[2 * h], carry[2 * h + 1]
            after = wrap_row(jnp.minimum(i + 1, lat_cells - 1), h)
            up = pltpu.roll(east * mine, 1, 1)
            dn = pltpu.roll(west * mine, LANE - 1, 1)
            at = pl.ds(aligned(top + i, LEV) + 8 * h, 8)
            total = center * mine + before + north_w * after
            total = total + jnp.where(lane8 == 0, 0.0, up) + jnp.where(lane8 == LANE - 1, 0.0, dn)
            force[at, last] = force[at, last] + total
            low = pl.ds(0, LANE)
            force[at, low] = force[at, low] + jnp.where(lane8 == 0, up, 0.0)
            high = pl.ds(lon_cells - LANE, LANE)
            force[at, high] = force[at, high] + jnp.where(lane8 == LANE - 1, dn, 0.0)
            handed += [south_w * mine, after]
        return tuple(handed)

    zero = jnp.zeros((8, LANE), F32)
    lax.fori_loop(0, lat_cells, wrap_step, (zero, wrap_row(0, 0), zero, wrap_row(0, 1)), unroll=4)
    for side, i in enumerate((0, lat_cells - 1)):
        for h in range(LEV // 8):
            lat_rows[pl.ds(LEV * side + 8 * h, 8), last] = wrap_row(i, h)
    table_copy.wait()
    lane8 = lanes8()
    dump = STEPS * lat_cells

    def entry(src, k):
        return table[src // 16, 8 * (src % 16) + k]

    def visit(src, _):
        q = got[src, pl.ds(0, NOTES), :].astype(I32).astype(F32)
        scales = scale_of(got[src, pl.ds(NOTES, 8), :].astype(I32).astype(F32))
        for nth in range(2):
            target = entry(src, nth)
            col = (target - 1) & (per_row - 1)
            row = jnp.where(target > 0, (target - 1) >> row_bits, dump)
            at = pl.ds(aligned(row, LEV), LEV)
            lanes = pl.ds(aligned(col, LANE), LANE)
            value = q[LEV * nth : LEV * nth + LEV] * scales[nth : nth + 1]
            force[at, lanes] = force[at, lanes] + value
        return 0

    lax.fori_loop(0, sources, visit, 0, unroll=8)
    own = own_group()
    in_low = (lane8 < 3)
    in_high = (lane8 >= LANE - 3)
    lanes = pl.ds(wide - LANE, LANE)

    def beside(src, _):
        @pl.when(entry(src, 7) > 0)
        def _():
            notes = got[src, pl.ds(NOTES, 8), :].astype(I32).astype(F32)
            base = jnp.broadcast_to(scale_of(notes[4:5]), (8, LANE))
            base = jnp.where(lane8 < 8, base, pltpu.roll(base, LANE - 16, 1))
            q = jnp.where(
                sublanes8() < 4,
                jnp.broadcast_to(notes[2:3], (8, LANE)),
                jnp.broadcast_to(notes[3:4], (8, LANE)),
            )
            q = shared_groups(jnp.where(own, q, 0.0))
            halves = [q * base, pltpu.roll(q, LANE - 16, 1) * base]
            for piece in range(PIECES):
                target = entry(src, 2 + piece)
                row = jnp.where(target > 0, target - 1, dump)
                at = aligned(row, LEV)
                for h, value in enumerate(halves if piece < 2 else halves[::-1]):
                    if piece == 1:
                        value = pltpu.roll(value, LANE - 4, 1)
                    if piece == 2:
                        value = pltpu.roll(value, 4, 1)
                    value = jnp.where(in_low if piece < 2 else in_high, value, 0.0)
                    where = pl.ds(at + 8 * h, 8)
                    force[where, lanes] = force[where, lanes] + value

        return 0

    lax.fori_loop(0, sources, beside, 0)
    lat_copy.wait()
    spread_copy.wait()
    n = 0
    for slot in (3, 2, 1):
        for d in range(slot):
            for side, (out, i) in enumerate(((south, lat_cells - 1 - d), (north, d))):
                out[pl.ds(LEV * n, LEV), :] = force[pl.ds((slot * lat_cells + i) * LEV, LEV), :]
            n += 1
    south[pl.ds(LEV * n, LEV), :] = lat_rows[pl.ds(LEV, LEV), :]
    north[pl.ds(LEV * n, LEV), :] = lat_rows[pl.ds(0, LEV), :]
    weight_at = LEV * (n + 1)
    sub = lax.broadcasted_iota(I32, (8, wide), 0)
    for d in range(3):
        for out, i in ((south, lat_cells - 1 - d), (north, d)):
            rows = jnp.zeros((8, wide), F32)
            for k in range(WEIGHTS):
                rows = jnp.where(sub == k, spread[pl.ds((i * WEIGHTS + k) * 8, 8), :], rows)
            out[pl.ds(weight_at + 8 * d, 8), :] = rows


def place(got, from_east, from_west, first, spread, lat_rows, fields, courant, lat_cells, per_row):
    wide = (per_row + 1) * LANE
    rim = (7 * LEV + 24, wide)

    def kernel(*refs):
        place_kernel(lat_cells, per_row, *refs)

    return pl.pallas_call(
        kernel,
        out_shape=[
            pltpu.VMEM(((STEPS * lat_cells + 1) * LEV, wide), F32),
            jax.ShapeDtypeStruct(rim, F32),
            jax.ShapeDtypeStruct(rim, F32),
            jax.ShapeDtypeStruct(lat_rows.shape, F32),
            pltpu.VMEM(spread.shape, F32),
        ],
        in_specs=[vmem_spec()] * 3 + [any_spec()] * 3,
        out_specs=[vmem_spec()] * 5,
        scratch_shapes=[
            pltpu.VMEM((8, LANE), I32),
            pltpu.VMEM((fields.shape[0], LANE), F32),
            pltpu.VMEM((courant.shape[0], LANE), F32),
            pltpu.SMEM((8, LANE), I32),
            pltpu.SemaphoreType.DMA((4,)),
        ],
        compiler_params=params(8),
        cost_estimate=pl.CostEstimate(flops=10**6, bytes_accessed=2 * 2**20, transcendentals=0),
        name="place_blocks",
    )(got, from_east, from_west, in_hbm(first), in_hbm(spread), in_hbm(lat_rows))


def steps_kernel(lat_cells, per_row, before, spread, force, out_hbm, result, sems):
    del before
    tiles = per_row + 1

    def at_of(slot, i, h):
        return pl.ds(pl.multiple_of((slot * lat_cells + i) * LEV, LEV) + 8 * h, 8)

    for slot in reversed(range(STEPS - 1)):

        def row_of(i, slot=slot):
            return {
                (h, c): force[at_of(slot + 1, i, h), pl.ds(c * LANE, LANE)]
                for h in range(LEV // 8)
                for c in range(tiles)
            }

        def force_of(i, h, c, slot=slot):
            return force[at_of(slot, i, h), pl.ds(c * LANE, LANE)]

        def finish(i, total, h, c, slot=slot):
            if slot or c < per_row:
                force[at_of(slot, i, h), pl.ds(c * LANE, LANE)] = total
            if slot == 0 and c < per_row:
                result[c, pl.ds(8 * h * lat_cells + i, 8, stride=lat_cells), :] = total

        sweep(lat_cells, tiles, spread, row_of, force_of, finish)
    writes = [
        pltpu.make_async_copy(result.at[c], out_hbm.at[:, pl.ds(c * LANE, LANE)], sems.at[c])
        for c in range(per_row)
    ]
    for write in writes:
        write.start()
    for write in writes:
        write.wait()


def steps(force, spread, lat_cells, per_row):
    lon_cells = per_row * LANE

    def kernel(*refs):
        steps_kernel(lat_cells, per_row, *refs)

    return pl.pallas_call(
        kernel,
        out_shape=[
            pltpu.VMEM(force.shape, F32),
            jax.ShapeDtypeStruct((LEV * lat_cells, lon_cells), F32),
        ],
        in_specs=[vmem_spec()] * 2,
        out_specs=[vmem_spec(), any_spec()],
        scratch_shapes=[
            pltpu.VMEM((per_row, LEV * lat_cells, LANE), F32),
            pltpu.SemaphoreType.DMA((per_row,)),
        ],
        input_output_aliases={0: 0},
        compiler_params=params(8),
        cost_estimate=pl.CostEstimate(
            flops=10 * STEPS * LEV * lat_cells * lon_cells, bytes_accessed=10 * 2**20, transcendentals=0
        ),
        name="interior_steps",
    )(force, spread)


def along_row(value, weights):
    wide = value.shape[1]
    return (
        weights[0] * value
        + pltpu.roll(weights[1] * value, 1, 1)
        + pltpu.roll(weights[2] * value, wide - 1, 1)
    )


def rim_kernel(
    lat_cells, per_row, before_hbm, from_north, from_south, force, lat_rows, spread, out_hbm, tiles, sems
):
    del before_hbm
    wide = force.shape[1]
    lon_cells = per_row * LANE
    weight_at = 7 * LEV
    writes = []
    for side, (halo, outer, inner) in enumerate(((from_north, 3, 4), (from_south, 4, 3))):

        def mine(q, side=side):
            return q if side == 0 else lat_cells - 1 - q

        def weight(q, d, halo=halo, mine=mine):
            if q < 0:
                row = halo[pl.ds(weight_at + 8 * (-1 - q), 8), :][d : d + 1]
                return jnp.broadcast_to(row, (LEV, wide))
            eight = spread[pl.ds((mine(q) * WEIGHTS + d) * 8, 8), :]
            return jnp.concatenate([eight, eight], axis=0)

        def sent(slot, q, halo=halo):
            first = {3: 0, 2: 3, 1: 5, 4: 6}[slot]
            return halo[pl.ds((first - 1 - q) * LEV, LEV), :]

        def inside(slot, q, side=side, mine=mine):
            if slot == STEPS:
                return lat_rows[pl.ds(LEV * side, LEV), :]
            return force[pl.ds((slot * lat_cells + mine(q)) * LEV, LEV), :]

        now = {}
        for step in range(1, STEPS + 1):
            slot = STEPS - step
            later = {}
            for q in range(-(STEPS - step), step):
                total = sent(slot, q) if q < 0 else None
                if step > 1 and q in now:
                    term = along_row(now[q], [weight(q, d) for d in range(3)])
                    total = term if total is None else total + term
                if step > 1 and q - 1 in now:
                    term = weight(q - 1, outer) * now[q - 1]
                    total = term if total is None else total + term
                if step == 1 and q == 0:
                    total = weight(-1, outer) * sent(STEPS, -1)
                if step > 1 and q + 1 in now:
                    total = total + weight(q + 1, inner) * now[q + 1]
                if q == -1:
                    total = total + weight(0, inner) * inside(slot + 1, 0)
                later[q] = total
            now = later
        for k in range(8):
            i = k if side == 0 else lat_cells - 8 + k
            row = force[pl.ds(i * LEV, LEV), pl.ds(0, lon_cells)]
            q = k if side == 0 else 7 - k
            if q < STEPS:
                row = row + now[q][:, :lon_cells]
            for c in range(per_row):
                tiles[side, c, pl.ds(k, LEV, stride=8), :] = row[:, c * LANE : (c + 1) * LANE]
        for c in range(per_row):
            write = pltpu.make_async_copy(
                tiles.at[side, c].reshape(LEV, 8, LANE),
                out_hbm.reshape(LEV, lat_cells, lon_cells).at[
                    :, pl.ds(0 if side == 0 else lat_cells - 8, 8), pl.ds(c * LANE, LANE)
                ],
                sems.at[per_row * side + c],
            )
            write.start()
            writes.append(write)
    for write in writes:
        write.wait()


def rim(result, from_north, from_south, force, lat_rows, spread, lat_cells, per_row):
    def kernel(*refs):
        rim_kernel(lat_cells, per_row, *refs)

    return pl.pallas_call(
        kernel,
        out_shape=jax.ShapeDtypeStruct(result.shape, F32),
        in_specs=[any_spec()] + [vmem_spec()] * 5,
        out_specs=any_spec(),
        scratch_shapes=[
            pltpu.VMEM((2, per_row, 8 * LEV, LANE), F32),
            pltpu.SemaphoreType.DMA((2 * per_row,)),
        ],
        input_output_aliases={0: 0},
        compiler_params=params(8),
        cost_estimate=pl.CostEstimate(flops=10**6, bytes_accessed=2 * 2**20, transcendentals=0),
        name="rim_rows",
    )(result, from_north, from_south, force, lat_rows, spread)


def on_device(
    op_blocks, innovations, obs_tiles, col_blocks, time_slots, obs_count, courant, later_adjoint
):
    lat_tiles = lax.axis_size("lat")
    lon_tiles = lax.axis_size("lon")
    devices = lat_tiles * lon_tiles
    levels, lat_cells, lon_cells = later_adjoint.shape
    per_row = lon_cells // LANE
    fields = later_adjoint.reshape(levels * lat_cells, lon_cells)
    weights = courant.reshape(courant.shape[0] * lat_cells, lon_cells)

    sent, to_east, to_west = contributions(
        op_blocks, innovations, obs_tiles, col_blocks, time_slots, obs_count,
        fields, weights, lat_cells, per_row, lon_tiles, devices,
    )
    eastward = [(i, (i + 1) % lon_tiles) for i in range(lon_tiles)]
    westward = [(j, i) for i, j in eastward]
    from_west = lax.ppermute(to_east, "lon", eastward)
    from_east = lax.ppermute(to_west, "lon", westward)
    got = lax.all_to_all(sent, ("lat", "lon"), split_axis=0, concat_axis=0, tiled=True)
    first, spread, lat_rows = ready(fields, weights, lat_cells, per_row)
    force, to_south, to_north, lat_rows, spread = place(
        got, from_east, from_west, first, spread, lat_rows, fields, weights, lat_cells, per_row
    )
    down = [(i, i + 1) for i in range(lat_tiles - 1)]
    up = [(j, i) for i, j in down]
    from_north = lax.ppermute(to_south, "lat", down)
    from_south = lax.ppermute(to_north, "lat", up)
    force, result = steps(force, spread, lat_cells, per_row)
    result = rim(result, from_north, from_south, force, lat_rows, spread, lat_cells, per_row)
    return result.reshape(levels, lat_cells, lon_cells)


def solution(mesh):
    in_specs = (
        P(("lat", "lon"), None, None),
        P(("lat", "lon"), None, None),
        P(("lat", "lon")),
        P(("lat", "lon")),
        P(("lat", "lon")),
        P(("lat", "lon")),
        P(None, "lat", "lon"),
        P(None, "lat", "lon"),
    )
    out_specs = P(None, "lat", "lon")
    return jax.shard_map(
        on_device, mesh=mesh, in_specs=in_specs, out_specs=out_specs, check_vma=False
    )
```

profile of v0, /device:TPU:1, one launch (start us, length us, event | category | flops | bytes accessed | tf_op | source)
XLA Modules:
  0.0 81.9 jit_solution(1474497639611280322)
XLA Ops:
  0.7 10.5 %contributions.1 = (s16[128,40,128]{2,1,0:T(8,128)(2,1)}, f32[48,128]{1,0:T(8,128)S(1)}, f32[48,128]{1,0:T(8,128)S(1)}) custom-call(s32[1]{0:T(128)S(6)} %copy.13.refs_0_, s32[128]{0:T(128)} %refs_1_.1, s32[128]{0:T(128)} %refs_2_.1, s32[128]{0:T(128)} %refs_3_.1, bf16[128,128,128]{2,1,0:T(8,128)(2,1)} %refs_4_.1, bf16[128,16,128]{2,1,0:T(8,128)(2,1)} %refs_5_.1, ...), custom_call_target="tpu_custom_call" | custom-call | flops 67108864 | bytes 6291456 | tf_op jit(solution)/shard_map/contributions/pallas_call | solution.py:223
  11.1 11.5 %all-to-all-start = ((s16[128,40,128]{2,1,0:T(8,128)(2,1)}), s16[128,40,128]{2,1,0:T(8,128)(2,1)S(1)}, u32[]{:S(2)}, u32[]{:S(2)}) async-start(s16[128,40,128]{2,1,0:T(8,128)(2,1)} %get-tuple-element.18), calls=%async_computation | async-start | bytes 2621440 | tf_op jit(solution)/shard_map/all_to_all | solution.py:763
  22.6 5.6 %collective-permute-start = (f32[48,128]{1,0:T(8,128)S(1)}, f32[48,128]{1,0:T(8,128)S(1)}, u32[]{:S(2)}, u32[]{:S(2)}) collective-permute-start(f32[48,128]{1,0:T(8,128)S(1)} %get-tuple-element.19), channel_id=1, source_target_pairs={{1,0},{2,1},{3,2},{4,3},{5,4},{6,5},{7,6},{8,7},{9,8},{10,9},{11,1... | collective-permute-start | bytes 73736 | tf_op jit(solution)/shard_map/ppermute | solution.py:762
  28.3 0.0 collective-permute-start.1
  28.3 7.0 %first_step.1 = (f32[1024,640]{1,0:T(8,128)}, f32[2560,640]{1,0:T(8,128)}, f32[32,640]{1,0:T(8,128)}) custom-call(f32[1024,512]{1,0:T(8,128)} %bitcast.4, f32[320,512]{1,0:T(8,128)} %bitcast.6), custom_call_target="tpu_custom_call" | custom-call | flops 10000000 | bytes 12582912 | tf_op jit(solution)/shard_map/first_step/pallas_call | solution.py:367
  35.2 0.0 collective-permute-done.refs_1_
  35.2 3.5 %collective-permute-done.1.refs_2_ = f32[48,128]{1,0:T(8,128)S(1)} collective-permute-done((f32[48,128]{1,0:T(8,128)S(1)}, f32[48,128]{1,0:T(8,128)S(1)}, u32[]{:S(2)}, u32[]{:S(2)}) %collective-permute-start.1) | collective-permute-done | bytes 24608 | tf_op jit(solution)/shard_map/ppermute | solution.py:761
  38.8 5.2 %all-to-all-done.refs_0_ = s16[128,40,128]{2,1,0:T(8,128)(2,1)S(1)} async-done(((s16[128,40,128]{2,1,0:T(8,128)(2,1)}), s16[128,40,128]{2,1,0:T(8,128)(2,1)S(1)}, u32[]{:S(2)}, u32[]{:S(2)}) %all-to-all-start) | async-done | bytes 1310752 | tf_op jit(solution)/shard_map/all_to_all | solution.py:763
  44.0 17.0 %place_blocks.1 = (f32[4112,640]{1,0:T(8,128)S(1)}, f32[136,640]{1,0:T(8,128)S(1)}, f32[136,640]{1,0:T(8,128)S(1)}, f32[32,640]{1,0:T(8,128)S(1)}, f32[2560,640]{1,0:T(8,128)S(1)}) custom-call(s16[128,40,128]{2,1,0:T(8,128)(2,1)S(1)} %all-to-all-done.refs_0_, f32[48,128]{1,0:T(8,128)S(1)} %collective-permute-done.refs_1_, ...), custom_call_target="tpu_custom_call" | custom-call | flops 1000000 | bytes 2097152 | tf_op jit(solution)/shard_map/place_blocks/pallas_call | solution.py:557
  61.0 5.4 %collective-permute-start.2 = (f32[136,640]{1,0:T(8,128)S(1)}, f32[136,640]{1,0:T(8,128)S(1)}, u32[]{:S(2)}, u32[]{:S(2)}) collective-permute-start(f32[136,640]{1,0:T(8,128)S(1)} %get-tuple-element.27), channel_id=1, source_target_pairs={{0,16},{16,32},{32,48},{48,64},{64,80},{80,96},{96,112},{1,17},{17... | collective-permute-start | bytes 1044488 | tf_op jit(solution)/shard_map/ppermute | solution.py:770
  66.4 1.9 %collective-permute-start.3 = (f32[136,640]{1,0:T(8,128)S(1)}, f32[136,640]{1,0:T(8,128)S(1)}, u32[]{:S(2)}, u32[]{:S(2)}) collective-permute-start(f32[136,640]{1,0:T(8,128)S(1)} %get-tuple-element.28), channel_id=1, source_target_pairs={{16,0},{32,16},{48,32},{64,48},{80,64},{96,80},{112,96},{17,1},{33... | collective-permute-start | bytes 1044488 | tf_op jit(solution)/shard_map/ppermute | solution.py:771
  68.3 12.0 %interior_steps.1 = (f32[4112,640]{1,0:T(8,128)S(1)}, f32[1024,512]{1,0:T(8,128)}) custom-call(f32[4112,640]{1,0:T(8,128)S(1)} %get-tuple-element.24.refs_0_, f32[2560,640]{1,0:T(8,128)S(1)} %get-tuple-element.25.refs_1_.refs_5_), custom_call_target="tpu_custom_call", output_to_operand_aliasing={{0}: (0, {})} | custom-call | flops 20971520 | bytes 10485760 | tf_op jit(solution)/shard_map/interior_steps/pallas_call | solution.py:623
  80.3 0.0 collective-permute-done.2.refs_1_
  80.3 0.0 collective-permute-done.3.refs_2_
  80.4 1.5 %rim_rows.1 = f32[1024,512]{1,0:T(8,128)} custom-call(f32[1024,512]{1,0:T(8,128)} %get-tuple-element.26.refs_0_, f32[136,640]{1,0:T(8,128)S(1)} %collective-permute-done.2.refs_1_, f32[136,640]{1,0:T(8,128)S(1)} %collective-permute-done.3.refs_2_, f32[4112,640]{1,0:T(8,128)S(1)} %get-tuple-element.29.refs_3_, ...), custom_call_target="tpu_custom_call", output_to_operand_aliasing={{}: (0, {})} | custom-call | flops 1000000 | bytes 2097152 | tf_op jit(solution)/shard_map/rim_rows/pallas_call | solution.py:728
Async XLA Ops:
  11.1 32.9 %all-to-all-start = ((s16[128,40,128]{2,1,0:T(8,128)(2,1)}), s16[128,40,128]{2,1,0:T(8,128)(2,1)S(1)}, u32[]{:S(2)}, u32[]{:S(2)}) async-start(s16[128,40,128]{2,1,0:T(8,128)(2,1)} %get-tuple-element.18), calls=%async_computation | async-start | bytes 2621440 | tf_op jit(solution)/shard_map/all_to_all | solution.py:763
  22.6 12.6 %collective-permute-start = (f32[48,128]{1,0:T(8,128)S(1)}, f32[48,128]{1,0:T(8,128)S(1)}, u32[]{:S(2)}, u32[]{:S(2)}) collective-permute-start(f32[48,128]{1,0:T(8,128)S(1)} %get-tuple-element.19), channel_id=1, source_target_pairs={{1,0},{2,1},{3,2},{4,3},{5,4},{6,5},{7,6},{8,7},{9,8},{10,9},{11,1... | collective-permute-start | bytes 73736 | tf_op jit(solution)/shard_map/ppermute | solution.py:762
  28.3 10.5 %collective-permute-start.1 = (f32[48,128]{1,0:T(8,128)S(1)}, f32[48,128]{1,0:T(8,128)S(1)}, u32[]{:S(2)}, u32[]{:S(2)}) collective-permute-start(f32[48,128]{1,0:T(8,128)S(1)} %get-tuple-element.20), channel_id=1, source_target_pairs={{0,1},{1,2},{2,3},{3,4},{4,5},{5,6},{6,7},{7,8},{8,9},{9,10},{10,1... | collective-permute-start | bytes 73736 | tf_op jit(solution)/shard_map/ppermute | solution.py:761
  61.0 19.3 %collective-permute-start.2 = (f32[136,640]{1,0:T(8,128)S(1)}, f32[136,640]{1,0:T(8,128)S(1)}, u32[]{:S(2)}, u32[]{:S(2)}) collective-permute-start(f32[136,640]{1,0:T(8,128)S(1)} %get-tuple-element.27), channel_id=1, source_target_pairs={{0,16},{16,32},{32,48},{48,64},{64,80},{80,96},{96,112},{1,17},{17... | collective-permute-start | bytes 1044488 | tf_op jit(solution)/shard_map/ppermute | solution.py:770
  66.4 13.9 %collective-permute-start.3 = (f32[136,640]{1,0:T(8,128)S(1)}, f32[136,640]{1,0:T(8,128)S(1)}, u32[]{:S(2)}, u32[]{:S(2)}) collective-permute-start(f32[136,640]{1,0:T(8,128)S(1)} %get-tuple-element.28), channel_id=1, source_target_pairs={{16,0},{32,16},{48,32},{64,48},{80,64},{96,80},{112,96},{17,1},{33... | collective-permute-start | bytes 1044488 | tf_op jit(solution)/shard_map/ppermute | solution.py:771
where the time goes:
time: 83 us; the launch traced here: 81.9 us
  Pallas kernels  47.9 us (58%)
  starting transfers between devices  24.4 us (29%)
  waiting for transfers between devices  8.75 us (11%)
    pallas_call x1, Pallas kernels, place(): pl.pallas_call(kernel, out_shape=[pltpu.VMEM(((STEPS * lat_cells + 1) * L...  17 us
    pallas_call x1, Pallas kernels, steps(): pl.pallas_call(kernel, out_shape=[pltpu.VMEM(force.shape, F32), jax.Shape...  12 us
    all_to_all x1, starting transfers between devices, on_device(): lax.all_to_all(sent, ('lat', 'lon'), split_axis=0, concat_axis=0, tiled=T...  11.5 us
    pallas_call x1, Pallas kernels, contributions(): pl.pallas_call(kernel, out_shape=[pltpu.HBM((devices, ROWS, LANE), I16),...  10.5 us
    pallas_call x1, Pallas kernels, ready(): pl.pallas_call(kernel, out_shape=[pltpu.HBM((lat_cells * LEV, wide), F32)...  6.95 us
    ppermute x1, starting transfers between devices, on_device(): from_east = lax.ppermute(to_west, 'lon', westward)  5.64 us
    ppermute x1, starting transfers between devices, on_device(): from_north = lax.ppermute(to_south, 'lat', down)  5.37 us
    all_to_all x1, waiting for transfers between devices, on_device(): lax.all_to_all(sent, ('lat', 'lon'), split_axis=0, concat_axis=0, tiled=T...  5.23 us
  transfers between devices with their start and end apart: 5, of which 2 were waited for; matrix products, arithmetic and copies ran while one was open for 0% of the time, Pallas kernels for 23%

commit v1 on v0

--- a/solution.py
+++ b/solution.py
@@ -200,7 +200,7 @@
             one(j)
             return 0
 
-        lax.fori_loop(part * chunk, (part + 1) * chunk, some, 0, unroll=8)
+        lax.fori_loop(part * chunk, (part + 1) * chunk, some, 0, unroll=32)
 
     def settle(d, _):
         pay[d, pl.ds(NOTES, 8), :] = meta[pl.ds(aligned(d, 8), 8), :].astype(I16)
@@ -302,7 +302,7 @@
         out.wait()
 
 
-def sweep(lat_cells, tiles, spread, row_of, force_of, finish, group_rows=8, wrap=False):
+def sweep(lat_cells, tiles, spread, row_of, force_of, finish, wrap=False):
     lane = lanes8()
     parts = [(h, c) for h in range(LEV // 8) for c in range(tiles)]
 
@@ -336,25 +336,11 @@
                 finish(i, seed, h, tiles)
         return handed
 
-    def rows(first, before, mine, number, ends):
-        for k in range(number):
-            after = None if ends and k == number - 1 else row_of(first + k + 1)
-            before = one_row(first + k, before, mine, after)
-            mine = after
-        return before, mine
-
-    def group(g, carry):
-        before, mine = (dict(zip(parts, values)) for values in carry)
-        before, mine = rows(g * group_rows, before, mine, group_rows, False)
-        return tuple(before[p] for p in parts), tuple(mine[p] for p in parts)
-
-    nothing = tuple(jnp.zeros((8, LANE), F32) for _ in parts)
-    first = row_of(0)
-    carry = lax.fori_loop(
-        0, lat_cells // group_rows - 1, group, (nothing, tuple(first[p] for p in parts))
-    )
-    before, mine = (dict(zip(parts, values)) for values in carry)
-    rows(lat_cells - group_rows, before, mine, group_rows, True)
+    before, mine = None, row_of(0)
+    for i in range(lat_cells):
+        after = row_of(i + 1) if i + 1 < lat_cells else None
+        before = one_row(i, before, mine, after)
+        mine = after
 
 
 def ready(fields, courant, lat_cells, per_row):
@@ -390,7 +376,7 @@
 def place_kernel(
     lat_cells, per_row, got, east_halo, west_halo, first_hbm, spread_hbm, lat_hbm,
     force, south, north, lat_rows, spread,
-    table_v, wrap_g, wrap_c, table, sems,
+    table_v, wrap_g, wrap_c, pieces, table, listed, sems,
 ):
     wide = (per_row + 1) * LANE
     lon_cells = per_row * LANE
@@ -439,6 +425,33 @@
                 spread[pl.ds(((8 * g + k) * WEIGHTS + d) * 8, 8), last] = jnp.broadcast_to(
                     eight[k : k + 1], (8, LANE)
                 )
+    own = own_group()
+    in_low = lane8 < 3
+    in_high = lane8 >= LANE - 3
+
+    def unpack(src, _):
+        notes = got[src, pl.ds(NOTES, 8), :].astype(I32).astype(F32)
+        base = jnp.broadcast_to(scale_of(notes[4:5]), (8, LANE))
+        base = jnp.where(lane8 < 8, base, pltpu.roll(base, LANE - 16, 1))
+        q = jnp.where(
+            sublanes8() < 4,
+            jnp.broadcast_to(notes[2:3], (8, LANE)),
+            jnp.broadcast_to(notes[3:4], (8, LANE)),
+        )
+        q = shared_groups(jnp.where(own, q, 0.0))
+        halves = [q * base, pltpu.roll(q, LANE - 16, 1) * base]
+        for piece in range(PIECES):
+            for h, value in enumerate(halves if piece < 2 else halves[::-1]):
+                if piece == 1:
+                    value = pltpu.roll(value, LANE - 4, 1)
+                if piece == 2:
+                    value = pltpu.roll(value, 4, 1)
+                value = jnp.where(in_low if piece < 2 else in_high, value, 0.0)
+                part = pl.ds(pl.multiple_of((src * PIECES + piece) * LEV, LEV) + 8 * h, 8)
+                pieces[part, :] = value
+        return 0
+
+    lax.fori_loop(0, sources, unpack, 0, unroll=16)
     first_copy.wait()
 
     def wrap_row(i, h):
@@ -468,7 +481,7 @@
         return tuple(handed)
 
     zero = jnp.zeros((8, LANE), F32)
-    lax.fori_loop(0, lat_cells, wrap_step, (zero, wrap_row(0, 0), zero, wrap_row(0, 1)), unroll=4)
+    lax.fori_loop(0, lat_cells, wrap_step, (zero, wrap_row(0, 0), zero, wrap_row(0, 1)), unroll=64)
     for side, i in enumerate((0, lat_cells - 1)):
         for h in range(LEV // 8):
             lat_rows[pl.ds(LEV * side + 8 * h, 8), last] = wrap_row(i, h)
@@ -476,57 +489,39 @@
     lane8 = lanes8()
     dump = STEPS * lat_cells
 
-    def entry(src, k):
-        return table[src // 16, 8 * (src % 16) + k]
-
-    def visit(src, _):
+    last_lanes = pl.ds(wide - LANE, LANE)
+    number = 0
+    for src in range(sources):
+
+        def entry(k, src=src):
+            return table[src // 16, 8 * (src % 16) + k]
+
         q = got[src, pl.ds(0, NOTES), :].astype(I32).astype(F32)
         scales = scale_of(got[src, pl.ds(NOTES, 8), :].astype(I32).astype(F32))
         for nth in range(2):
-            target = entry(src, nth)
+            target = entry(nth)
             col = (target - 1) & (per_row - 1)
             row = jnp.where(target > 0, (target - 1) >> row_bits, dump)
             at = pl.ds(aligned(row, LEV), LEV)
             lanes = pl.ds(aligned(col, LANE), LANE)
             value = q[LEV * nth : LEV * nth + LEV] * scales[nth : nth + 1]
             force[at, lanes] = force[at, lanes] + value
+        for piece in range(PIECES):
+            target = entry(2 + piece)
+            listed[number] = target + ((src * PIECES + piece) << 10)
+            number = number + jnp.minimum(target, 1)
+    for k in range(8):
+        listed[number + k] = dump + 1
+
+    def beside(group, _):
+        for k in range(8):
+            item = listed[8 * group + k]
+            part = pl.ds(aligned(item >> 10, LEV), LEV)
+            at = pl.ds(aligned((item & 1023) - 1, LEV), LEV)
+            force[at, last_lanes] = force[at, last_lanes] + pieces[part, :]
         return 0
 
-    lax.fori_loop(0, sources, visit, 0, unroll=8)
-    own = own_group()
-    in_low = (lane8 < 3)
-    in_high = (lane8 >= LANE - 3)
-    lanes = pl.ds(wide - LANE, LANE)
-
-    def beside(src, _):
-        @pl.when(entry(src, 7) > 0)
-        def _():
-            notes = got[src, pl.ds(NOTES, 8), :].astype(I32).astype(F32)
-            base = jnp.broadcast_to(scale_of(notes[4:5]), (8, LANE))
-            base = jnp.where(lane8 < 8, base, pltpu.roll(base, LANE - 16, 1))
-            q = jnp.where(
-                sublanes8() < 4,
-                jnp.broadcast_to(notes[2:3], (8, LANE)),
-                jnp.broadcast_to(notes[3:4], (8, LANE)),
-            )
-            q = shared_groups(jnp.where(own, q, 0.0))
-            halves = [q * base, pltpu.roll(q, LANE - 16, 1) * base]
-            for piece in range(PIECES):
-                target = entry(src, 2 + piece)
-                row = jnp.where(target > 0, target - 1, dump)
-                at = aligned(row, LEV)
-                for h, value in enumerate(halves if piece < 2 else halves[::-1]):
-                    if piece == 1:
-                        value = pltpu.roll(value, LANE - 4, 1)
-                    if piece == 2:
-                        value = pltpu.roll(value, 4, 1)
-                    value = jnp.where(in_low if piece < 2 else in_high, value, 0.0)
-                    where = pl.ds(at + 8 * h, 8)
-                    force[where, lanes] = force[where, lanes] + value
-
-        return 0
-
-    lax.fori_loop(0, sources, beside, 0)
+    lax.fori_loop(0, (number + 7) >> 3, beside, 0)
     lat_copy.wait()
     spread_copy.wait()
     n = 0
@@ -569,10 +564,12 @@
             pltpu.VMEM((8, LANE), I32),
             pltpu.VMEM((fields.shape[0], LANE), F32),
             pltpu.VMEM((courant.shape[0], LANE), F32),
+            pltpu.VMEM((got.shape[0] * PIECES * LEV, LANE), F32),
             pltpu.SMEM((8, LANE), I32),
+            pltpu.SMEM((got.shape[0] * PIECES + 8,), I32),
             pltpu.SemaphoreType.DMA((4,)),
         ],
-        compiler_params=params(8),
+        compiler_params=params(12),
         cost_estimate=pl.CostEstimate(flops=10**6, bytes_accessed=2 * 2**20, transcendentals=0),
         name="place_blocks",
     )(got, from_east, from_west, in_hbm(first), in_hbm(spread), in_hbm(lat_rows))

time: 83 us -> 62.1 us (0.75); the launches traced: 81.9 us -> 61.9 us
  Pallas kernels: 47.9 us -> 28.9 us
  starting transfers between devices: 24.4 us -> 23.1 us
    pallas_call x1, Pallas kernels: 17 us -> 6.38 us  [place(): pl.pallas_call(kernel, out_shape=[pltpu.VMEM(((STEPS * lat_cells + 1) * L...]
    pallas_call x1, Pallas kernels: 12 us -> 7.19 us  [steps(): pl.pallas_call(kernel, out_shape=[pltpu.VMEM(force.shape, F32), jax.Shape...]
    pallas_call x1, Pallas kernels: 10.5 us -> 7.12 us  [contributions(): pl.pallas_call(kernel, out_shape=[pltpu.HBM((devices, ROWS, LANE), I16),...]
    ppermute x1, starting transfers between devices: 5.37 us -> 3.82 us  [on_device(): from_north = lax.ppermute(to_south, 'lat', down)]
  transfers between devices with their start and end apart: 5 -> 5, of which waited for: 2 -> 2; matrix products, arithmetic and copies ran while one was open for 0% -> 0% of each run, Pallas kernels for 23% -> 22%
where the time goes in v1:
time: 62.1 us; the launch traced here: 61.9 us
  Pallas kernels  28.9 us (47%)
  starting transfers between devices  23.1 us (37%)
  waiting for transfers between devices  9.02 us (15%)
  between operations  0.89 us (1%)
    all_to_all x1, starting transfers between devices, on_device(): lax.all_to_all(sent, ('lat', 'lon'), split_axis=0, concat_axis=0, tiled=T...  11.5 us
    pallas_call x1, Pallas kernels, steps(): pl.pallas_call(kernel, out_shape=[pltpu.VMEM(force.shape, F32), jax.Shape...  7.19 us
    pallas_call x1, Pallas kernels, contributions(): pl.pallas_call(kernel, out_shape=[pltpu.HBM((devices, ROWS, LANE), I16),...  7.12 us
    pallas_call x1, Pallas kernels, ready(): pl.pallas_call(kernel, out_shape=[pltpu.HBM((lat_cells * LEV, wide), F32)...  6.68 us
    pallas_call x1, Pallas kernels, place(): pl.pallas_call(kernel, out_shape=[pltpu.VMEM(((STEPS * lat_cells + 1) * L...  6.38 us
    ppermute x1, starting transfers between devices, on_device(): from_east = lax.ppermute(to_west, 'lon', westward)  5.64 us
    all_to_all x1, waiting for transfers between devices, on_device(): lax.all_to_all(sent, ('lat', 'lon'), split_axis=0, concat_axis=0, tiled=T...  5.23 us
    ppermute x1, starting transfers between devices, on_device(): from_north = lax.ppermute(to_south, 'lat', down)  3.82 us
  transfers between devices with their start and end apart: 5, of which 2 were waited for; matrix products, arithmetic and copies ran while one was open for 0% of the time, Pallas kernels for 22%

profile of v1, /device:TPU:1, one launch (start us, length us, event | category | flops | bytes accessed | tf_op | source)
XLA Modules:
  0.0 61.9 jit_solution(13070795851059728642)
XLA Ops:
  0.7 7.1 %contributions.1 = (s16[128,40,128]{2,1,0:T(8,128)(2,1)}, f32[48,128]{1,0:T(8,128)S(1)}, f32[48,128]{1,0:T(8,128)S(1)}) custom-call(s32[1]{0:T(128)S(6)} %copy.13.refs_0_, s32[128]{0:T(128)} %refs_1_.1, s32[128]{0:T(128)} %refs_2_.1, s32[128]{0:T(128)} %refs_3_.1, bf16[128,128,128]{2,1,0:T(8,128)(2,1)} %refs_4_.1, bf16[128,16,128]{2,1,0:T(8,128)(2,1)} %refs_5_.1, ...), custom_call_target="tpu_custom_call" | custom-call | flops 67108864 | bytes 6291456 | tf_op jit(solution)/shard_map/contributions/pallas_call | solution.py:223
  7.8 11.5 %all-to-all-start = ((s16[128,40,128]{2,1,0:T(8,128)(2,1)}), s16[128,40,128]{2,1,0:T(8,128)(2,1)S(1)}, u32[]{:S(2)}, u32[]{:S(2)}) async-start(s16[128,40,128]{2,1,0:T(8,128)(2,1)} %get-tuple-element.18), calls=%async_computation | async-start | bytes 2621440 | tf_op jit(solution)/shard_map/all_to_all | solution.py:760
  19.3 5.6 %collective-permute-start = (f32[48,128]{1,0:T(8,128)S(1)}, f32[48,128]{1,0:T(8,128)S(1)}, u32[]{:S(2)}, u32[]{:S(2)}) collective-permute-start(f32[48,128]{1,0:T(8,128)S(1)} %get-tuple-element.19), channel_id=1, source_target_pairs={{1,0},{2,1},{3,2},{4,3},{5,4},{6,5},{7,6},{8,7},{9,8},{10,9},{11,1... | collective-permute-start | bytes 73736 | tf_op jit(solution)/shard_map/ppermute | solution.py:759
  24.9 0.0 collective-permute-start.1
  24.9 6.7 %first_step.1 = (f32[1024,640]{1,0:T(8,128)}, f32[2560,640]{1,0:T(8,128)}, f32[32,640]{1,0:T(8,128)}) custom-call(f32[1024,512]{1,0:T(8,128)} %bitcast.4, f32[320,512]{1,0:T(8,128)} %bitcast.6), custom_call_target="tpu_custom_call" | custom-call | flops 10000000 | bytes 12582912 | tf_op jit(solution)/shard_map/first_step/pallas_call | solution.py:353
  31.6 0.0 collective-permute-done.refs_1_
  31.6 3.8 %collective-permute-done.1.refs_2_ = f32[48,128]{1,0:T(8,128)S(1)} collective-permute-done((f32[48,128]{1,0:T(8,128)S(1)}, f32[48,128]{1,0:T(8,128)S(1)}, u32[]{:S(2)}, u32[]{:S(2)}) %collective-permute-start.1) | collective-permute-done | bytes 24608 | tf_op jit(solution)/shard_map/ppermute | solution.py:758
  35.4 5.2 %all-to-all-done.refs_0_ = s16[128,40,128]{2,1,0:T(8,128)(2,1)S(1)} async-done(((s16[128,40,128]{2,1,0:T(8,128)(2,1)}), s16[128,40,128]{2,1,0:T(8,128)(2,1)S(1)}, u32[]{:S(2)}, u32[]{:S(2)}) %all-to-all-start) | async-done | bytes 1310752 | tf_op jit(solution)/shard_map/all_to_all | solution.py:760
  40.6 6.4 %place_blocks.1 = (f32[4112,640]{1,0:T(8,128)S(1)}, f32[136,640]{1,0:T(8,128)S(1)}, f32[136,640]{1,0:T(8,128)S(1)}, f32[32,640]{1,0:T(8,128)S(1)}, f32[2560,640]{1,0:T(8,128)S(1)}) custom-call(s16[128,40,128]{2,1,0:T(8,128)(2,1)S(1)} %all-to-all-done.refs_0_, f32[48,128]{1,0:T(8,128)S(1)} %collective-permute-done.refs_1_, ...), custom_call_target="tpu_custom_call" | custom-call | flops 1000000 | bytes 2097152 | tf_op jit(solution)/shard_map/place_blocks/pallas_call | solution.py:552
  47.0 3.8 %collective-permute-start.2 = (f32[136,640]{1,0:T(8,128)S(1)}, f32[136,640]{1,0:T(8,128)S(1)}, u32[]{:S(2)}, u32[]{:S(2)}) collective-permute-start(f32[136,640]{1,0:T(8,128)S(1)} %get-tuple-element.27), channel_id=1, source_target_pairs={{0,16},{16,32},{32,48},{48,64},{64,80},{80,96},{96,112},{1,17},{17... | collective-permute-start | bytes 1044488 | tf_op jit(solution)/shard_map/ppermute | solution.py:767
  50.9 2.1 %collective-permute-start.3 = (f32[136,640]{1,0:T(8,128)S(1)}, f32[136,640]{1,0:T(8,128)S(1)}, u32[]{:S(2)}, u32[]{:S(2)}) collective-permute-start(f32[136,640]{1,0:T(8,128)S(1)} %get-tuple-element.28), channel_id=1, source_target_pairs={{16,0},{32,16},{48,32},{64,48},{80,64},{96,80},{112,96},{17,1},{33... | collective-permute-start | bytes 1044488 | tf_op jit(solution)/shard_map/ppermute | solution.py:768
  53.0 7.2 %interior_steps.1 = (f32[4112,640]{1,0:T(8,128)S(1)}, f32[1024,512]{1,0:T(8,128)}) custom-call(f32[4112,640]{1,0:T(8,128)S(1)} %get-tuple-element.24.refs_0_, f32[2560,640]{1,0:T(8,128)S(1)} %get-tuple-element.25.refs_1_.refs_5_), custom_call_target="tpu_custom_call", output_to_operand_aliasing={{0}: (0, {})} | custom-call | flops 20971520 | bytes 10485760 | tf_op jit(solution)/shard_map/interior_steps/pallas_call | solution.py:620
  60.2 0.0 collective-permute-done.2.refs_1_
  60.2 0.0 collective-permute-done.3.refs_2_
  60.2 1.5 %rim_rows.1 = f32[1024,512]{1,0:T(8,128)} custom-call(f32[1024,512]{1,0:T(8,128)} %get-tuple-element.26.refs_0_, f32[136,640]{1,0:T(8,128)S(1)} %collective-permute-done.2.refs_1_, f32[136,640]{1,0:T(8,128)S(1)} %collective-permute-done.3.refs_2_, f32[4112,640]{1,0:T(8,128)S(1)} %get-tuple-element.29.refs_3_, ...), custom_call_target="tpu_custom_call", output_to_operand_aliasing={{}: (0, {})} | custom-call | flops 1000000 | bytes 2097152 | tf_op jit(solution)/shard_map/rim_rows/pallas_call | solution.py:725
Async XLA Ops:
  7.8 32.9 %all-to-all-start = ((s16[128,40,128]{2,1,0:T(8,128)(2,1)}), s16[128,40,128]{2,1,0:T(8,128)(2,1)S(1)}, u32[]{:S(2)}, u32[]{:S(2)}) async-start(s16[128,40,128]{2,1,0:T(8,128)(2,1)} %get-tuple-element.18), calls=%async_computation | async-start | bytes 2621440 | tf_op jit(solution)/shard_map/all_to_all | solution.py:760
  19.3 12.3 %collective-permute-start = (f32[48,128]{1,0:T(8,128)S(1)}, f32[48,128]{1,0:T(8,128)S(1)}, u32[]{:S(2)}, u32[]{:S(2)}) collective-permute-start(f32[48,128]{1,0:T(8,128)S(1)} %get-tuple-element.19), channel_id=1, source_target_pairs={{1,0},{2,1},{3,2},{4,3},{5,4},{6,5},{7,6},{8,7},{9,8},{10,9},{11,1... | collective-permute-start | bytes 73736 | tf_op jit(solution)/shard_map/ppermute | solution.py:759
  24.9 10.5 %collective-permute-start.1 = (f32[48,128]{1,0:T(8,128)S(1)}, f32[48,128]{1,0:T(8,128)S(1)}, u32[]{:S(2)}, u32[]{:S(2)}) collective-permute-start(f32[48,128]{1,0:T(8,128)S(1)} %get-tuple-element.20), channel_id=1, source_target_pairs={{0,1},{1,2},{2,3},{3,4},{4,5},{5,6},{6,7},{7,8},{8,9},{9,10},{10,1... | collective-permute-start | bytes 73736 | tf_op jit(solution)/shard_map/ppermute | solution.py:758
  47.0 13.1 %collective-permute-start.2 = (f32[136,640]{1,0:T(8,128)S(1)}, f32[136,640]{1,0:T(8,128)S(1)}, u32[]{:S(2)}, u32[]{:S(2)}) collective-permute-start(f32[136,640]{1,0:T(8,128)S(1)} %get-tuple-element.27), channel_id=1, source_target_pairs={{0,16},{16,32},{32,48},{48,64},{64,80},{80,96},{96,112},{1,17},{17... | collective-permute-start | bytes 1044488 | tf_op jit(solution)/shard_map/ppermute | solution.py:767
  50.9 9.3 %collective-permute-start.3 = (f32[136,640]{1,0:T(8,128)S(1)}, f32[136,640]{1,0:T(8,128)S(1)}, u32[]{:S(2)}, u32[]{:S(2)}) collective-permute-start(f32[136,640]{1,0:T(8,128)S(1)} %get-tuple-element.28), channel_id=1, source_target_pairs={{16,0},{32,16},{48,32},{64,48},{80,64},{96,80},{112,96},{17,1},{33... | collective-permute-start | bytes 1044488 | tf_op jit(solution)/shard_map/ppermute | solution.py:768

commit v2 on v1

--- a/solution.py
+++ b/solution.py
@@ -105,7 +105,7 @@
                 sems.at[6 + parts + 2 * side],
             )
         )
-    for copy in small + strips + [inn_copy] + copies:
+    for copy in small + [inn_copy] + copies + strips:
         copy.start()
 
     def clear(d, _):
@@ -117,20 +117,6 @@
     lane8 = lanes8()
     lane = lane8[0:1]
     own = own_group()
-
-    for copy in strips:
-        copy.wait()
-    total = (rows + extra) // 8
-    for v in range(-(-total // PACK)):
-        east = jnp.zeros((8, LANE), F32)
-        west = jnp.zeros((8, LANE), F32)
-        for k in range(min(PACK, total - v * PACK)):
-            at = pl.ds(8 * (v * PACK + k), 8)
-            here = lane8 // HALO == k
-            west = jnp.where(here, pltpu.roll(strip[0, at, :], HALO * k, 1), west)
-            east = jnp.where(here, pltpu.roll(strip[1, at, :], (HALO * k + HALO) % LANE, 1), east)
-        to_east[pl.ds(8 * v, 8), :] = east
-        to_west[pl.ds(8 * v, 8), :] = west
 
     for copy in small:
         copy.wait()
@@ -202,14 +188,33 @@
 
         lax.fori_loop(part * chunk, (part + 1) * chunk, some, 0, unroll=32)
 
-    def settle(d, _):
-        pay[d, pl.ds(NOTES, 8), :] = meta[pl.ds(aligned(d, 8), 8), :].astype(I16)
-        return 0
-
-    lax.fori_loop(0, devices, settle, 0, unroll=8)
-    out_copy = pltpu.make_async_copy(pay, sent, sems.at[0])
-    out_copy.start()
-    out_copy.wait()
+    outs = []
+    share = devices // parts
+    for part in range(parts):
+
+        def settle(d, _):
+            pay[d, pl.ds(NOTES, 8), :] = meta[pl.ds(aligned(d, 8), 8), :].astype(I16)
+            return 0
+
+        lax.fori_loop(part * share, (part + 1) * share, settle, 0, unroll=share)
+        at = pl.ds(part * share, share)
+        outs.append(pltpu.make_async_copy(pay.at[at], sent.at[at], sems.at[part]))
+        outs[-1].start()
+    for copy in strips:
+        copy.wait()
+    total = (rows + extra) // 8
+    for v in range(-(-total // PACK)):
+        east = jnp.zeros((8, LANE), F32)
+        west = jnp.zeros((8, LANE), F32)
+        for k in range(min(PACK, total - v * PACK)):
+            at = pl.ds(8 * (v * PACK + k), 8)
+            group = lane8 // HALO
+            west = jnp.where(group == k, pltpu.roll(strip[0, at, :], HALO * k, 1), west)
+            east = jnp.where(group == (k - 1) % PACK, pltpu.roll(strip[1, at, :], HALO * k, 1), east)
+        to_east[pl.ds(8 * v, 8), :] = east
+        to_west[pl.ds(8 * v, 8), :] = west
+    for out in outs:
+        out.wait()
 
 
 def contributions(op_blocks, innovations, obs_tiles, col_blocks, time_slots, obs_count, fields, courant, lat_cells, per_row, lon_tiles, devices):
@@ -285,13 +290,13 @@
         }
 
     def finish(i, total, h, c):
-        first[pl.ds(aligned(i, LEV) + 8 * h, 8), pl.ds(c * LANE, LANE)] = total
+        first[pl.ds(i * LEV + 8 * h, 8), pl.ds(c * LANE, LANE)] = total
 
     for side, i in enumerate((0, lat_cells - 1)):
         row = row_of(i)
         for h, c in parts:
             lat_rows[pl.ds(LEV * side + 8 * h, 8), pl.ds(c * LANE, LANE)] = row[h, c]
-    sweep(lat_cells, per_row, spread, row_of, None, finish, wrap=True)
+    sweep(lat_cells, per_row + 1, per_row, spread, row_of, None, finish)
     outs = [
         pltpu.make_async_copy(first, first_hbm, sems.at[1]),
         pltpu.make_async_copy(lat_rows, lat_hbm.at[:, pl.ds(0, per_row * LANE)], sems.at[2]),
@@ -302,38 +307,42 @@
         out.wait()
 
 
-def sweep(lat_cells, tiles, spread, row_of, force_of, finish, wrap=False):
+def sweep(lat_cells, tiles, given, spread, row_of, force_of, finish, row_done=None):
     lane = lanes8()
-    parts = [(h, c) for h in range(LEV // 8) for c in range(tiles)]
+    halves = range(LEV // 8)
 
     def weight_of(i, d):
-        at = pl.ds(pl.multiple_of((i * WEIGHTS + d) * 8, 8), 8)
-        return [spread[at, pl.ds(c * LANE, LANE)] for c in range(tiles)]
+        at = pl.ds((i * WEIGHTS + d) * 8, 8)
+        return [spread[at, pl.ds(c * LANE, LANE)] for c in range(given)]
 
     def one_row(i, before, mine, after):
         center, east, west, south = (weight_of(i, d) for d in range(4))
         north = weight_of(i + 1, 4) if after is not None else None
         handed = {}
-        for h in range(LEV // 8):
-            up = [pltpu.roll(east[c] * mine[h, c], 1, 1) for c in range(tiles)]
-            dn = [pltpu.roll(west[c] * mine[h, c], LANE - 1, 1) for c in range(tiles)]
+        for h in halves:
+            up = [east[c] * mine[h, c] for c in range(given)]
+            dn = [west[c] * mine[h, c] for c in range(given)]
             for c in range(tiles):
+                if c == given:
+                    total = jnp.where(lane == LANE - 1, up[c - 1], 0.0)
+                    total = pltpu.roll(total, 1, 1)
+                    other = jnp.where(lane == 0, dn[0], 0.0)
+                    finish(i, total + pltpu.roll(other, LANE - 1, 1), h, c)
+                    continue
+                left = 0.0 if given < tiles and c == 0 else up[c - 1]
+                right = 0.0 if given < tiles and c == given - 1 else dn[(c + 1) % given]
                 total = center[c] * mine[h, c]
-                left = 0.0 if wrap and c == 0 else up[c - 1]
-                right = 0.0 if wrap and c == tiles - 1 else dn[(c + 1) % tiles]
-                total = total + jnp.where(lane == 0, left, up[c])
-                total = total + jnp.where(lane == LANE - 1, right, dn[c])
+                total = total + pltpu.roll(jnp.where(lane == LANE - 1, left, up[c]), 1, 1)
+                total = total + pltpu.roll(jnp.where(lane == 0, right, dn[c]), LANE - 1, 1)
                 if force_of is not None:
                     total = total + force_of(i, h, c)
                 if before is not None:
                     total = total + before[h, c]
                 if after is not None:
                     total = total + north[c] * after[h, c]
+                finish(i, total, h, c)
+            for c in range(given):
                 handed[h, c] = south[c] * mine[h, c]
-                finish(i, total, h, c)
-            if wrap:
-                seed = jnp.where(lane == 0, up[tiles - 1], jnp.where(lane == LANE - 1, dn[0], 0.0))
-                finish(i, seed, h, tiles)
         return handed
 
     before, mine = None, row_of(0)
@@ -341,6 +350,8 @@
         after = row_of(i + 1) if i + 1 < lat_cells else None
         before = one_row(i, before, mine, after)
         mine = after
+        if row_done is not None:
+            row_done(i)
 
 
 def ready(fields, courant, lat_cells, per_row):
@@ -410,9 +421,9 @@
     for n in range(rows + extra):
         v, k = divmod(n, PACK)
         at = pl.ds(8 * v, 8)
-        low = pltpu.roll(east_halo[at, :], (-HALO * k) % LANE, 1)
-        high = pltpu.roll(west_halo[at, :], (-HALO * k - HALO) % LANE, 1)
-        wrap = jnp.where(lane8 < HALO, low, jnp.where(lane8 >= LANE - HALO, high, 0.0))
+        both = jnp.where(lane8 // HALO == k, east_halo[at, :], west_halo[at, :])
+        both = pltpu.roll(both, (-HALO * k) % LANE, 1)
+        wrap = jnp.where((lane8 < HALO) | (lane8 >= LANE - HALO), both, 0.0)
         if n < rows:
             wrap_g[pl.ds(8 * n, 8), :] = wrap
         else:
@@ -579,8 +590,12 @@
     del before
     tiles = per_row + 1
 
+    writes = []
+    lon_cells = per_row * LANE
+    out_rows = out_hbm.reshape(LEV, lat_cells, lon_cells)
+
     def at_of(slot, i, h):
-        return pl.ds(pl.multiple_of((slot * lat_cells + i) * LEV, LEV) + 8 * h, 8)
+        return pl.ds((slot * lat_cells + i) * LEV + 8 * h, 8)
 
     for slot in reversed(range(STEPS - 1)):
 
@@ -595,18 +610,27 @@
             return force[at_of(slot, i, h), pl.ds(c * LANE, LANE)]
 
         def finish(i, total, h, c, slot=slot):
-            if slot or c < per_row:
+            if slot or i < 8 or i >= lat_cells - 8:
                 force[at_of(slot, i, h), pl.ds(c * LANE, LANE)] = total
-            if slot == 0 and c < per_row:
+            else:
                 result[c, pl.ds(8 * h * lat_cells + i, 8, stride=lat_cells), :] = total
 
-        sweep(lat_cells, tiles, spread, row_of, force_of, finish)
-    writes = [
-        pltpu.make_async_copy(result.at[c], out_hbm.at[:, pl.ds(c * LANE, LANE)], sems.at[c])
-        for c in range(per_row)
-    ]
-    for write in writes:
-        write.start()
+        def row_done(i):
+            if i % 16 == 7 and i > 8:
+                rows = pl.ds(i - 15, 16)
+                for c in range(per_row):
+                    write = pltpu.make_async_copy(
+                        result.at[c].reshape(LEV, lat_cells, LANE).at[:, rows],
+                        out_rows.at[:, rows, pl.ds(c * LANE, LANE)],
+                        sems.at[len(writes)],
+                    )
+                    write.start()
+                    writes.append(write)
+
+        sweep(
+            lat_cells, tiles if slot else per_row, tiles, spread, row_of, force_of, finish,
+            None if slot else row_done,
+        )
     for write in writes:
         write.wait()
 
@@ -627,7 +651,7 @@
         out_specs=[vmem_spec(), any_spec()],
         scratch_shapes=[
             pltpu.VMEM((per_row, LEV * lat_cells, LANE), F32),
-            pltpu.SemaphoreType.DMA((per_row,)),
+            pltpu.SemaphoreType.DMA((per_row * (lat_cells // 16),)),
         ],
         input_output_aliases={0: 0},
         compiler_params=params(8),

time: 62.1 us -> 60.7 us (0.977)
  Pallas kernels: 28.9 us -> 27 us
    pallas_call x1, Pallas kernels: 7.19 us -> 6.11 us  [steps(): pl.pallas_call(kernel, out_shape=[pltpu.VMEM(force.shape, F32), jax.Shape...]
  transfers between devices with their start and end apart: 5 -> 5, of which waited for: 2 -> 3; matrix products, arithmetic and copies ran while one was open for 0% -> 0% of each run, Pallas kernels for 22% -> 21%
where the time goes in v2:
time: 60.7 us; the launch traced here: 60.4 us
  Pallas kernels  27 us (44%)
  starting transfers between devices  23 us (38%)
  waiting for transfers between devices  9.54 us (16%)
  between operations  0.89 us (1%)
    all_to_all x1, starting transfers between devices, on_device(): lax.all_to_all(sent, ('lat', 'lon'), split_axis=0, concat_axis=0, tiled=T...  11.5 us
    pallas_call x1, Pallas kernels, contributions(): pl.pallas_call(kernel, out_shape=[pltpu.HBM((devices, ROWS, LANE), I16),...  6.57 us
    pallas_call x1, Pallas kernels, ready(): pl.pallas_call(kernel, out_shape=[pltpu.HBM((lat_cells * LEV, wide), F32)...  6.54 us
    pallas_call x1, Pallas kernels, place(): pl.pallas_call(kernel, out_shape=[pltpu.VMEM(((STEPS * lat_cells + 1) * L...  6.27 us
    pallas_call x1, Pallas kernels, steps(): pl.pallas_call(kernel, out_shape=[pltpu.VMEM(force.shape, F32), jax.Shape...  6.11 us
    ppermute x1, starting transfers between devices, on_device(): from_east = lax.ppermute(to_west, 'lon', westward)  5.64 us
    all_to_all x1, waiting for transfers between devices, on_device(): lax.all_to_all(sent, ('lat', 'lon'), split_axis=0, concat_axis=0, tiled=T...  5.23 us
    ppermute x1, waiting for transfers between devices, on_device(): from_west = lax.ppermute(to_east, 'lon', eastward)  3.93 us
  transfers between devices with their start and end apart: 5, of which 3 were waited for; matrix products, arithmetic and copies ran while one was open for 0% of the time, Pallas kernels for 21%

profile of v2, /device:TPU:1, one launch (start us, length us, event | category | flops | bytes accessed | tf_op | source)
XLA Modules:
  0.0 60.4 jit_solution(12521624496372818815)
XLA Ops:
  0.7 6.6 %contributions.1 = (s16[128,40,128]{2,1,0:T(8,128)(2,1)}, f32[48,128]{1,0:T(8,128)S(1)}, f32[48,128]{1,0:T(8,128)S(1)}) custom-call(s32[1]{0:T(128)S(6)} %copy.13.refs_0_, s32[128]{0:T(128)} %refs_1_.1, s32[128]{0:T(128)} %refs_2_.1, s32[128]{0:T(128)} %refs_3_.1, bf16[128,128,128]{2,1,0:T(8,128)(2,1)} %refs_4_.1, bf16[128,16,128]{2,1,0:T(8,128)(2,1)} %refs_5_.1, ...), custom_call_target="tpu_custom_call" | custom-call | flops 67108864 | bytes 6291456 | tf_op jit(solution)/shard_map/contributions/pallas_call | solution.py:228
  7.2 11.5 %all-to-all-start = ((s16[128,40,128]{2,1,0:T(8,128)(2,1)}), s16[128,40,128]{2,1,0:T(8,128)(2,1)S(1)}, u32[]{:S(2)}, u32[]{:S(2)}) async-start(s16[128,40,128]{2,1,0:T(8,128)(2,1)} %get-tuple-element.18), calls=%async_computation | async-start | bytes 2621440 | tf_op jit(solution)/shard_map/all_to_all | solution.py:784
  18.7 5.6 %collective-permute-start = (f32[48,128]{1,0:T(8,128)S(1)}, f32[48,128]{1,0:T(8,128)S(1)}, u32[]{:S(2)}, u32[]{:S(2)}) collective-permute-start(f32[48,128]{1,0:T(8,128)S(1)} %get-tuple-element.19), channel_id=1, source_target_pairs={{1,0},{2,1},{3,2},{4,3},{5,4},{6,5},{7,6},{8,7},{9,8},{10,9},{11,1... | collective-permute-start | bytes 73736 | tf_op jit(solution)/shard_map/ppermute | solution.py:783
  24.4 0.0 collective-permute-start.1
  24.4 6.5 %first_step.1 = (f32[1024,640]{1,0:T(8,128)}, f32[2560,640]{1,0:T(8,128)}, f32[32,640]{1,0:T(8,128)}) custom-call(f32[1024,512]{1,0:T(8,128)} %bitcast.4, f32[320,512]{1,0:T(8,128)} %bitcast.6), custom_call_target="tpu_custom_call" | custom-call | flops 10000000 | bytes 12582912 | tf_op jit(solution)/shard_map/first_step/pallas_call | solution.py:364
  30.9 0.0 collective-permute-done.refs_1_
  30.9 3.9 %collective-permute-done.1.refs_2_ = f32[48,128]{1,0:T(8,128)S(1)} collective-permute-done((f32[48,128]{1,0:T(8,128)S(1)}, f32[48,128]{1,0:T(8,128)S(1)}, u32[]{:S(2)}, u32[]{:S(2)}) %collective-permute-start.1) | collective-permute-done | bytes 24608 | tf_op jit(solution)/shard_map/ppermute | solution.py:782
  34.9 5.2 %all-to-all-done.refs_0_ = s16[128,40,128]{2,1,0:T(8,128)(2,1)S(1)} async-done(((s16[128,40,128]{2,1,0:T(8,128)(2,1)}), s16[128,40,128]{2,1,0:T(8,128)(2,1)S(1)}, u32[]{:S(2)}, u32[]{:S(2)}) %all-to-all-start) | async-done | bytes 1310752 | tf_op jit(solution)/shard_map/all_to_all | solution.py:784
  40.1 6.3 %place_blocks.1 = (f32[4112,640]{1,0:T(8,128)S(1)}, f32[136,640]{1,0:T(8,128)S(1)}, f32[136,640]{1,0:T(8,128)S(1)}, f32[32,640]{1,0:T(8,128)S(1)}, f32[2560,640]{1,0:T(8,128)S(1)}) custom-call(s16[128,40,128]{2,1,0:T(8,128)(2,1)S(1)} %all-to-all-done.refs_0_, f32[48,128]{1,0:T(8,128)S(1)} %collective-permute-done.refs_1_, ...), custom_call_target="tpu_custom_call" | custom-call | flops 1000000 | bytes 2097152 | tf_op jit(solution)/shard_map/place_blocks/pallas_call | solution.py:563
  46.4 3.8 %collective-permute-start.2 = (f32[136,640]{1,0:T(8,128)S(1)}, f32[136,640]{1,0:T(8,128)S(1)}, u32[]{:S(2)}, u32[]{:S(2)}) collective-permute-start(f32[136,640]{1,0:T(8,128)S(1)} %get-tuple-element.27), channel_id=1, source_target_pairs={{0,16},{16,32},{32,48},{48,64},{64,80},{80,96},{96,112},{1,17},{17... | collective-permute-start | bytes 1044488 | tf_op jit(solution)/shard_map/ppermute | solution.py:791
  50.2 2.1 %collective-permute-start.3 = (f32[136,640]{1,0:T(8,128)S(1)}, f32[136,640]{1,0:T(8,128)S(1)}, u32[]{:S(2)}, u32[]{:S(2)}) collective-permute-start(f32[136,640]{1,0:T(8,128)S(1)} %get-tuple-element.28), channel_id=1, source_target_pairs={{16,0},{32,16},{48,32},{64,48},{80,64},{96,80},{112,96},{17,1},{33... | collective-permute-start | bytes 1044488 | tf_op jit(solution)/shard_map/ppermute | solution.py:792
  52.3 6.1 %interior_steps.1 = (f32[4112,640]{1,0:T(8,128)S(1)}, f32[1024,512]{1,0:T(8,128)}) custom-call(f32[4112,640]{1,0:T(8,128)S(1)} %get-tuple-element.24.refs_0_, f32[2560,640]{1,0:T(8,128)S(1)} %get-tuple-element.25.refs_1_.refs_5_), custom_call_target="tpu_custom_call", output_to_operand_aliasing={{0}: (0, {})} | custom-call | flops 20971520 | bytes 10485760 | tf_op jit(solution)/shard_map/interior_steps/pallas_call | solution.py:644
  58.4 0.0 collective-permute-done.2.refs_1_
  58.4 0.4 collective-permute-done.3.refs_2_
  58.8 1.5 %rim_rows.1 = f32[1024,512]{1,0:T(8,128)} custom-call(f32[1024,512]{1,0:T(8,128)} %get-tuple-element.26.refs_0_, f32[136,640]{1,0:T(8,128)S(1)} %collective-permute-done.2.refs_1_, f32[136,640]{1,0:T(8,128)S(1)} %collective-permute-done.3.refs_2_, f32[4112,640]{1,0:T(8,128)S(1)} %get-tuple-element.29.refs_3_, ...), custom_call_target="tpu_custom_call", output_to_operand_aliasing={{}: (0, {})} | custom-call | flops 1000000 | bytes 2097152 | tf_op jit(solution)/shard_map/rim_rows/pallas_call | solution.py:749
Async XLA Ops:
  7.2 32.9 %all-to-all-start = ((s16[128,40,128]{2,1,0:T(8,128)(2,1)}), s16[128,40,128]{2,1,0:T(8,128)(2,1)S(1)}, u32[]{:S(2)}, u32[]{:S(2)}) async-start(s16[128,40,128]{2,1,0:T(8,128)(2,1)} %get-tuple-element.18), calls=%async_computation | async-start | bytes 2621440 | tf_op jit(solution)/shard_map/all_to_all | solution.py:784
  18.7 12.2 %collective-permute-start = (f32[48,128]{1,0:T(8,128)S(1)}, f32[48,128]{1,0:T(8,128)S(1)}, u32[]{:S(2)}, u32[]{:S(2)}) collective-permute-start(f32[48,128]{1,0:T(8,128)S(1)} %get-tuple-element.19), channel_id=1, source_target_pairs={{1,0},{2,1},{3,2},{4,3},{5,4},{6,5},{7,6},{8,7},{9,8},{10,9},{11,1... | collective-permute-start | bytes 73736 | tf_op jit(solution)/shard_map/ppermute | solution.py:783
  24.4 10.5 %collective-permute-start.1 = (f32[48,128]{1,0:T(8,128)S(1)}, f32[48,128]{1,0:T(8,128)S(1)}, u32[]{:S(2)}, u32[]{:S(2)}) collective-permute-start(f32[48,128]{1,0:T(8,128)S(1)} %get-tuple-element.20), channel_id=1, source_target_pairs={{0,1},{1,2},{2,3},{3,4},{4,5},{5,6},{6,7},{7,8},{8,9},{9,10},{10,1... | collective-permute-start | bytes 73736 | tf_op jit(solution)/shard_map/ppermute | solution.py:782
  46.4 12.0 %collective-permute-start.2 = (f32[136,640]{1,0:T(8,128)S(1)}, f32[136,640]{1,0:T(8,128)S(1)}, u32[]{:S(2)}, u32[]{:S(2)}) collective-permute-start(f32[136,640]{1,0:T(8,128)S(1)} %get-tuple-element.27), channel_id=1, source_target_pairs={{0,16},{16,32},{32,48},{48,64},{64,80},{80,96},{96,112},{1,17},{17... | collective-permute-start | bytes 1044488 | tf_op jit(solution)/shard_map/ppermute | solution.py:791
  50.2 8.6 %collective-permute-start.3 = (f32[136,640]{1,0:T(8,128)S(1)}, f32[136,640]{1,0:T(8,128)S(1)}, u32[]{:S(2)}, u32[]{:S(2)}) collective-permute-start(f32[136,640]{1,0:T(8,128)S(1)} %get-tuple-element.28), channel_id=1, source_target_pairs={{16,0},{32,16},{48,32},{64,48},{80,64},{96,80},{112,96},{17,1},{33... | collective-permute-start | bytes 1044488 | tf_op jit(solution)/shard_map/ppermute | solution.py:792

commit v3 on v2

--- a/solution.py
+++ b/solution.py
@@ -386,7 +386,7 @@
 
 def place_kernel(
     lat_cells, per_row, got, east_halo, west_halo, first_hbm, spread_hbm, lat_hbm,
-    force, south, north, lat_rows, spread,
+    force, near, far, lat_rows, spread,
     table_v, wrap_g, wrap_c, pieces, table, listed, sems,
 ):
     wide = (per_row + 1) * LANE
@@ -535,22 +535,31 @@
     lax.fori_loop(0, (number + 7) >> 3, beside, 0)
     lat_copy.wait()
     spread_copy.wait()
+    odd = lax.axis_index("lat") % 2 == 1
+
+    def hand(at, to_south, to_north):
+        near[at, :] = jnp.where(odd, to_north, to_south)
+        far[at, :] = jnp.where(odd, to_south, to_north)
+
     n = 0
     for slot in (3, 2, 1):
         for d in range(slot):
-            for side, (out, i) in enumerate(((south, lat_cells - 1 - d), (north, d))):
-                out[pl.ds(LEV * n, LEV), :] = force[pl.ds((slot * lat_cells + i) * LEV, LEV), :]
+            to_south, to_north = (
+                force[pl.ds((slot * lat_cells + i) * LEV, LEV), :] for i in (lat_cells - 1 - d, d)
+            )
+            hand(pl.ds(LEV * n, LEV), to_south, to_north)
             n += 1
-    south[pl.ds(LEV * n, LEV), :] = lat_rows[pl.ds(LEV, LEV), :]
-    north[pl.ds(LEV * n, LEV), :] = lat_rows[pl.ds(0, LEV), :]
+    hand(pl.ds(LEV * n, LEV), lat_rows[pl.ds(LEV, LEV), :], lat_rows[pl.ds(0, LEV), :])
     weight_at = LEV * (n + 1)
     sub = lax.broadcasted_iota(I32, (8, wide), 0)
     for d in range(3):
-        for out, i in ((south, lat_cells - 1 - d), (north, d)):
+        both = []
+        for i in (lat_cells - 1 - d, d):
             rows = jnp.zeros((8, wide), F32)
             for k in range(WEIGHTS):
                 rows = jnp.where(sub == k, spread[pl.ds((i * WEIGHTS + k) * 8, 8), :], rows)
-            out[pl.ds(weight_at + 8 * d, 8), :] = rows
+            both.append(rows)
+        hand(pl.ds(weight_at + 8 * d, 8), *both)
 
 
 def place(got, from_east, from_west, first, spread, lat_rows, fields, courant, lat_cells, per_row):
@@ -672,28 +681,33 @@
 
 
 def rim_kernel(
-    lat_cells, per_row, before_hbm, from_north, from_south, force, lat_rows, spread, out_hbm, tiles, sems
+    lat_cells, per_row, before_hbm, near, far, force, lat_rows, spread, out_hbm, tiles, sems
 ):
     del before_hbm
     wide = force.shape[1]
     lon_cells = per_row * LANE
     weight_at = 7 * LEV
     writes = []
-    for side, (halo, outer, inner) in enumerate(((from_north, 3, 4), (from_south, 4, 3))):
+    odd = lax.axis_index("lat") % 2 == 1
+    for side, (outer, inner) in enumerate(((3, 4), (4, 3))):
+
+        def halo(at, side=side):
+            one, other = near[at, :], far[at, :]
+            return jnp.where(odd, one, other) if side == 0 else jnp.where(odd, other, one)
 
         def mine(q, side=side):
             return q if side == 0 else lat_cells - 1 - q
 
         def weight(q, d, halo=halo, mine=mine):
             if q < 0:
-                row = halo[pl.ds(weight_at + 8 * (-1 - q), 8), :][d : d + 1]
+                row = halo(pl.ds(weight_at + 8 * (-1 - q), 8))[d : d + 1]
                 return jnp.broadcast_to(row, (LEV, wide))
             eight = spread[pl.ds((mine(q) * WEIGHTS + d) * 8, 8), :]
             return jnp.concatenate([eight, eight], axis=0)
 
         def sent(slot, q, halo=halo):
             first = {3: 0, 2: 3, 1: 5, 4: 6}[slot]
-            return halo[pl.ds((first - 1 - q) * LEV, LEV), :]
+            return halo(pl.ds((first - 1 - q) * LEV, LEV))
 
         def inside(slot, q, side=side, mine=mine):
             if slot == STEPS:
@@ -742,7 +756,7 @@
         write.wait()
 
 
-def rim(result, from_north, from_south, force, lat_rows, spread, lat_cells, per_row):
+def rim(result, near, far, force, lat_rows, spread, lat_cells, per_row):
     def kernel(*refs):
         rim_kernel(lat_cells, per_row, *refs)
 
@@ -759,7 +773,7 @@
         compiler_params=params(8),
         cost_estimate=pl.CostEstimate(flops=10**6, bytes_accessed=2 * 2**20, transcendentals=0),
         name="rim_rows",
-    )(result, from_north, from_south, force, lat_rows, spread)
+    )(result, near, far, force, lat_rows, spread)
 
 
 def on_device(
@@ -783,15 +797,16 @@
     from_east = lax.ppermute(to_west, "lon", westward)
     got = lax.all_to_all(sent, ("lat", "lon"), split_axis=0, concat_axis=0, tiled=True)
     first, spread, lat_rows = ready(fields, weights, lat_cells, per_row)
-    force, to_south, to_north, lat_rows, spread = place(
+    force, near, far, lat_rows, spread = place(
         got, from_east, from_west, first, spread, lat_rows, fields, weights, lat_cells, per_row
     )
-    down = [(i, i + 1) for i in range(lat_tiles - 1)]
-    up = [(j, i) for i, j in down]
-    from_north = lax.ppermute(to_south, "lat", down)
-    from_south = lax.ppermute(to_north, "lat", up)
+    pairs = [(i, i + 1) for i in range(lat_tiles - 1)]
+    inner = [pair for i, j in pairs[0::2] for pair in ((i, j), (j, i))]
+    outer = [pair for i, j in pairs[1::2] for pair in ((i, j), (j, i))]
+    far = lax.ppermute(far, "lat", outer)
+    near = lax.ppermute(near, "lat", inner)
     force, result = steps(force, spread, lat_cells, per_row)
-    result = rim(result, from_north, from_south, force, lat_rows, spread, lat_cells, per_row)
+    result = rim(result, near, far, force, lat_rows, spread, lat_cells, per_row)
     return result.reshape(levels, lat_cells, lon_cells)
 
 

time: 60.7 us -> 58.6 us (0.965)
  starting transfers between devices: 23 us -> 21.3 us
    ppermute x2, starting transfers between devices: 5.88 us -> 4.13 us  [the longest x1 2.36 us: on_device(): far = lax.ppermute(far, 'lat', outer)]
  transfers between devices with their start and end apart: 5 -> 5, of which waited for: 3 -> 3; matrix products, arithmetic and copies ran while one was open for 0% -> 0% of each run, Pallas kernels for 21% -> 22%
where the time goes in v3:
time: 58.6 us; the launch traced here: 58.4 us
  Pallas kernels  27 us (46%)
  starting transfers between devices  21.3 us (36%)
  waiting for transfers between devices  9.27 us (16%)
  between operations  0.88 us (2%)
    all_to_all x1, starting transfers between devices, on_device(): lax.all_to_all(sent, ('lat', 'lon'), split_axis=0, concat_axis=0, tiled=T...  11.5 us
    pallas_call x1, Pallas kernels, contributions(): pl.pallas_call(kernel, out_shape=[pltpu.HBM((devices, ROWS, LANE), I16),...  6.57 us
    pallas_call x1, Pallas kernels, ready(): pl.pallas_call(kernel, out_shape=[pltpu.HBM((lat_cells * LEV, wide), F32)...  6.54 us
    pallas_call x1, Pallas kernels, place(): pl.pallas_call(kernel, out_shape=[pltpu.VMEM(((STEPS * lat_cells + 1) * L...  6.24 us
    pallas_call x1, Pallas kernels, steps(): pl.pallas_call(kernel, out_shape=[pltpu.VMEM(force.shape, F32), jax.Shape...  6.11 us
    ppermute x1, starting transfers between devices, on_device(): from_east = lax.ppermute(to_west, 'lon', westward)  5.64 us
    all_to_all x1, waiting for transfers between devices, on_device(): lax.all_to_all(sent, ('lat', 'lon'), split_axis=0, concat_axis=0, tiled=T...  5.23 us
    ppermute x1, waiting for transfers between devices, on_device(): from_west = lax.ppermute(to_east, 'lon', eastward)  3.93 us
  transfers between devices with their start and end apart: 5, of which 3 were waited for; matrix products, arithmetic and copies ran while one was open for 0% of the time, Pallas kernels for 22%

profile of v3, /device:TPU:1, one launch (start us, length us, event | category | flops | bytes accessed | tf_op | source)
XLA Modules:
  0.0 58.4 jit_solution(13838225944413120333)
XLA Ops:
  0.7 6.6 %contributions.1 = (s16[128,40,128]{2,1,0:T(8,128)(2,1)}, f32[48,128]{1,0:T(8,128)S(1)}, f32[48,128]{1,0:T(8,128)S(1)}) custom-call(s32[1]{0:T(128)S(6)} %copy.13.refs_0_, s32[128]{0:T(128)} %refs_1_.1, s32[128]{0:T(128)} %refs_2_.1, s32[128]{0:T(128)} %refs_3_.1, bf16[128,128,128]{2,1,0:T(8,128)(2,1)} %refs_4_.1, bf16[128,16,128]{2,1,0:T(8,128)(2,1)} %refs_5_.1, ...), custom_call_target="tpu_custom_call" | custom-call | flops 67108864 | bytes 6291456 | tf_op jit(solution)/shard_map/contributions/pallas_call | solution.py:228
  7.2 11.5 %all-to-all-start = ((s16[128,40,128]{2,1,0:T(8,128)(2,1)}), s16[128,40,128]{2,1,0:T(8,128)(2,1)S(1)}, u32[]{:S(2)}, u32[]{:S(2)}) async-start(s16[128,40,128]{2,1,0:T(8,128)(2,1)} %get-tuple-element.18), calls=%async_computation | async-start | bytes 2621440 | tf_op jit(solution)/shard_map/all_to_all | solution.py:798
  18.7 5.6 %collective-permute-start = (f32[48,128]{1,0:T(8,128)S(1)}, f32[48,128]{1,0:T(8,128)S(1)}, u32[]{:S(2)}, u32[]{:S(2)}) collective-permute-start(f32[48,128]{1,0:T(8,128)S(1)} %get-tuple-element.19), channel_id=1, source_target_pairs={{1,0},{2,1},{3,2},{4,3},{5,4},{6,5},{7,6},{8,7},{9,8},{10,9},{11,1... | collective-permute-start | bytes 73736 | tf_op jit(solution)/shard_map/ppermute | solution.py:797
  24.4 0.0 collective-permute-start.1
  24.4 6.5 %first_step.1 = (f32[1024,640]{1,0:T(8,128)}, f32[2560,640]{1,0:T(8,128)}, f32[32,640]{1,0:T(8,128)}) custom-call(f32[1024,512]{1,0:T(8,128)} %bitcast.4, f32[320,512]{1,0:T(8,128)} %bitcast.6), custom_call_target="tpu_custom_call" | custom-call | flops 10000000 | bytes 12582912 | tf_op jit(solution)/shard_map/first_step/pallas_call | solution.py:364
  30.9 0.0 collective-permute-done.refs_1_
  30.9 3.9 %collective-permute-done.1.refs_2_ = f32[48,128]{1,0:T(8,128)S(1)} collective-permute-done((f32[48,128]{1,0:T(8,128)S(1)}, f32[48,128]{1,0:T(8,128)S(1)}, u32[]{:S(2)}, u32[]{:S(2)}) %collective-permute-start.1) | collective-permute-done | bytes 24608 | tf_op jit(solution)/shard_map/ppermute | solution.py:796
  34.9 5.2 %all-to-all-done.refs_0_ = s16[128,40,128]{2,1,0:T(8,128)(2,1)S(1)} async-done(((s16[128,40,128]{2,1,0:T(8,128)(2,1)}), s16[128,40,128]{2,1,0:T(8,128)(2,1)S(1)}, u32[]{:S(2)}, u32[]{:S(2)}) %all-to-all-start) | async-done | bytes 1310752 | tf_op jit(solution)/shard_map/all_to_all | solution.py:798
  40.1 6.2 %place_blocks.1 = (f32[4112,640]{1,0:T(8,128)S(1)}, f32[136,640]{1,0:T(8,128)S(1)}, f32[136,640]{1,0:T(8,128)S(1)}, f32[32,640]{1,0:T(8,128)S(1)}, f32[2560,640]{1,0:T(8,128)S(1)}) custom-call(s16[128,40,128]{2,1,0:T(8,128)(2,1)S(1)} %all-to-all-done.refs_0_, f32[48,128]{1,0:T(8,128)S(1)} %collective-permute-done.refs_1_, ...), custom_call_target="tpu_custom_call" | custom-call | flops 1000000 | bytes 2097152 | tf_op jit(solution)/shard_map/place_blocks/pallas_call | solution.py:572
  46.3 1.8 %collective-permute-start.2 = (f32[136,640]{1,0:T(8,128)S(1)}, f32[136,640]{1,0:T(8,128)S(1)}, u32[]{:S(2)}, u32[]{:S(2)}) collective-permute-start(f32[136,640]{1,0:T(8,128)S(1)} %get-tuple-element.27), channel_id=1, source_target_pairs={{0,16},{16,0},{32,48},{48,32},{64,80},{80,64},{96,112},{112,96},{1... | collective-permute-start | bytes 1044488 | tf_op jit(solution)/shard_map/ppermute | solution.py:807
  48.1 2.4 %collective-permute-start.3 = (f32[136,640]{1,0:T(8,128)S(1)}, f32[136,640]{1,0:T(8,128)S(1)}, u32[]{:S(2)}, u32[]{:S(2)}) collective-permute-start(f32[136,640]{1,0:T(8,128)S(1)} %get-tuple-element.28), channel_id=1, source_target_pairs={{16,32},{32,16},{48,64},{64,48},{80,96},{96,80},{17,33},{33,17},{4... | collective-permute-start | bytes 1044488 | tf_op jit(solution)/shard_map/ppermute | solution.py:806
  50.5 6.1 %interior_steps.1 = (f32[4112,640]{1,0:T(8,128)S(1)}, f32[1024,512]{1,0:T(8,128)}) custom-call(f32[4112,640]{1,0:T(8,128)S(1)} %get-tuple-element.24.refs_0_, f32[2560,640]{1,0:T(8,128)S(1)} %get-tuple-element.25.refs_1_.refs_5_), custom_call_target="tpu_custom_call", output_to_operand_aliasing={{0}: (0, {})} | custom-call | flops 20971520 | bytes 10485760 | tf_op jit(solution)/shard_map/interior_steps/pallas_call | solution.py:653
  56.6 0.0 collective-permute-done.2.refs_1_
  56.6 0.1 collective-permute-done.3.refs_2_
  56.7 1.5 %rim_rows.1 = f32[1024,512]{1,0:T(8,128)} custom-call(f32[1024,512]{1,0:T(8,128)} %get-tuple-element.26.refs_0_, f32[136,640]{1,0:T(8,128)S(1)} %collective-permute-done.2.refs_1_, f32[136,640]{1,0:T(8,128)S(1)} %collective-permute-done.3.refs_2_, f32[4112,640]{1,0:T(8,128)S(1)} %get-tuple-element.29.refs_3_, ...), custom_call_target="tpu_custom_call", output_to_operand_aliasing={{}: (0, {})} | custom-call | flops 1000000 | bytes 2097152 | tf_op jit(solution)/shard_map/rim_rows/pallas_call | solution.py:763
Async XLA Ops:
  7.2 32.9 %all-to-all-start = ((s16[128,40,128]{2,1,0:T(8,128)(2,1)}), s16[128,40,128]{2,1,0:T(8,128)(2,1)S(1)}, u32[]{:S(2)}, u32[]{:S(2)}) async-start(s16[128,40,128]{2,1,0:T(8,128)(2,1)} %get-tuple-element.18), calls=%async_computation | async-start | bytes 2621440 | tf_op jit(solution)/shard_map/all_to_all | solution.py:798
  18.7 12.2 %collective-permute-start = (f32[48,128]{1,0:T(8,128)S(1)}, f32[48,128]{1,0:T(8,128)S(1)}, u32[]{:S(2)}, u32[]{:S(2)}) collective-permute-start(f32[48,128]{1,0:T(8,128)S(1)} %get-tuple-element.19), channel_id=1, source_target_pairs={{1,0},{2,1},{3,2},{4,3},{5,4},{6,5},{7,6},{8,7},{9,8},{10,9},{11,1... | collective-permute-start | bytes 73736 | tf_op jit(solution)/shard_map/ppermute | solution.py:797
  24.4 10.5 %collective-permute-start.1 = (f32[48,128]{1,0:T(8,128)S(1)}, f32[48,128]{1,0:T(8,128)S(1)}, u32[]{:S(2)}, u32[]{:S(2)}) collective-permute-start(f32[48,128]{1,0:T(8,128)S(1)} %get-tuple-element.20), channel_id=1, source_target_pairs={{0,1},{1,2},{2,3},{3,4},{4,5},{5,6},{6,7},{7,8},{8,9},{9,10},{10,1... | collective-permute-start | bytes 73736 | tf_op jit(solution)/shard_map/ppermute | solution.py:796
  46.3 10.3 %collective-permute-start.2 = (f32[136,640]{1,0:T(8,128)S(1)}, f32[136,640]{1,0:T(8,128)S(1)}, u32[]{:S(2)}, u32[]{:S(2)}) collective-permute-start(f32[136,640]{1,0:T(8,128)S(1)} %get-tuple-element.27), channel_id=1, source_target_pairs={{0,16},{16,0},{32,48},{48,32},{64,80},{80,64},{96,112},{112,96},{1... | collective-permute-start | bytes 1044488 | tf_op jit(solution)/shard_map/ppermute | solution.py:807
  48.1 8.6 %collective-permute-start.3 = (f32[136,640]{1,0:T(8,128)S(1)}, f32[136,640]{1,0:T(8,128)S(1)}, u32[]{:S(2)}, u32[]{:S(2)}) collective-permute-start(f32[136,640]{1,0:T(8,128)S(1)} %get-tuple-element.28), channel_id=1, source_target_pairs={{16,32},{32,16},{48,64},{64,48},{80,96},{96,80},{17,33},{33,17},{4... | collective-permute-start | bytes 1044488 | tf_op jit(solution)/shard_map/ppermute | solution.py:806
